TPU v7x, 256 devices: a whole 4x4x8 slice. The times are simulated.
256 devices in a mesh: ctx: 64 (over y, z, core), head: 4 (over x).
Axes of the slice: x: 4, y: 4, z: 8, core: 2. Of those that a mesh axis runs over, the one named last changes fastest.
Arguments:
- query_nope: bfloat16 [2, 32, 8192], P(None, None, 'head'), may hold values from -12 to 12
- query_rope: bfloat16 [2, 32, 4096], P(None, None, 'head'), may hold values from -9 to 9
- key_up: bfloat16 [64, 128, 512], P('head'), may hold values from -0.5 to 0.5
- cache_latent: bfloat16 [131072, 512], P('ctx'), may hold values from -6 to 6
- cache_rope: bfloat16 [65536, 128], P('ctx'), may hold values from -6 to 6
- chosen_blocks: int32 [2, 32, 16], replicated, may hold values from 0 to 1023, as said below
- value_up: bfloat16 [64, 512, 128], P('head', 'ctx'), may hold values from -0.25 to 0.25
- output_weight: bfloat16 [8192, 7168], P('head', 'ctx'), may hold values from -0.25 to 0.25
Outputs:
- attention_out: bfloat16 [2, 32, 7168], P(None, 'head', 'ctx')
Inputs may be any that keep to these rules, and one draw needn't show every extreme that they name: `chosen_blocks`: each row names 16 different blocks at each step. In each step, the blocks i * 16 to (i + 1) * 16 - 1 are named at most 24 times over all rows, and exactly 24 times for some i.
All inputs are finite; a program needn't handle non-finite values.
Results may differ from a plain program's by a relative error of at most 0.0078.
Values may be sent and summed in bfloat16 or wider, within the bound.
No kernel may reach another device: no remote copies, remote signals or barrier semaphores. Data moves between devices by JAX's collectives and lax.ppermute only.
A program may use at most 384 MiB of HBM per device.

v0:
```python
import jax
import jax.numpy as jnp
from jax import lax
from jax.sharding import PartitionSpec as P

BLOCK = 128


very_low = -1e30


def project_values(latent_part, value_float):
    return jnp.einsum("rhl,hlv->rhv", latent_part, value_float, precision=lax.Precision.HIGHEST)


def attend_rows(
    query_latent,
    query_rot,
    chosen,
    cache_latent,
    cache_rope,
    value_float,
    output_weight,
    capacity,
    step_count,
    score_scale,
):
    row_count, pick_count = chosen.shape
    latent_width = cache_latent.shape[1]
    rope_width = cache_rope.shape[1] // 2
    blocks_here = cache_latent.shape[0] // BLOCK
    device = lax.axis_index("ctx")
    flat_mine = (chosen // blocks_here == device).reshape(-1)
    flat_chosen = chosen.reshape(-1)
    pair_order = jnp.argsort(jnp.where(flat_mine, 0, 1).astype(jnp.int32), stable=True)[:capacity]
    pair_valid = flat_mine[pair_order]
    pair_row = pair_order // pick_count
    pair_block = jnp.where(pair_valid, flat_chosen[pair_order] - device * blocks_here, 0)
    latent_blocks = cache_latent.reshape(blocks_here, BLOCK, latent_width)[pair_block]
    rope_blocks = cache_rope.reshape(blocks_here, BLOCK, rope_width)[pair_block]
    pair_latent = query_latent[pair_row]
    pair_rot = query_rot[pair_row]
    scores = jnp.einsum(
        "phl,pbl->phb", pair_latent, latent_blocks, preferred_element_type=jnp.float32
    )
    scores = (
        scores
        + jnp.einsum("phd,pbd->phb", pair_rot, rope_blocks, preferred_element_type=jnp.float32)
    ) * score_scale
    block_peak = jnp.max(scores, axis=-1)
    shifted = jnp.exp(scores - block_peak[..., None])
    weights = shifted.astype(jnp.bfloat16)
    block_sum = jnp.sum(shifted, axis=-1)
    block_out = jnp.einsum(
        "phb,pbl->phl", weights, latent_blocks, preferred_element_type=jnp.float32
    )
    block_peak = jnp.where(pair_valid[:, None], block_peak, very_low)
    member = (pair_row[None, :] == jnp.arange(row_count, dtype=jnp.int32)[:, None]) & pair_valid[
        None, :
    ]
    local_peak = jnp.max(jnp.where(member[:, :, None], block_peak[None], very_low), axis=1)
    member_float = member.astype(jnp.float32)
    row_top = lax.pmax(local_peak, "ctx")
    factor = jnp.where(pair_valid[:, None], jnp.exp(block_peak - row_top[pair_row]), 0.0)
    merged = jnp.einsum(
        "rp,phl->rhl", member_float, factor[..., None] * block_out, precision=lax.Precision.HIGHEST
    )
    row_total = jnp.dot(member_float, factor * block_sum, precision=lax.Precision.HIGHEST)
    merged, row_total = (merged, row_total)
    own_share = lax.psum_scatter(merged, "ctx", scatter_dimension=2, tiled=True)
    partial_value = project_values(own_share, value_float)
    head_sum, row_total = lax.psum((partial_value, row_total), "ctx")
    head_rows = (head_sum / row_total[..., None]).astype(jnp.bfloat16).reshape(row_count, -1)
    projected = jnp.dot(head_rows, output_weight, preferred_element_type=jnp.float32)
    projected = projected.reshape(step_count, row_count // step_count, projected.shape[1])
    return lax.psum_scatter(projected, "head", scatter_dimension=1, tiled=True).astype(jnp.bfloat16)


def body(
    query_nope, query_rope, key_up, cache_latent, cache_rope, chosen_blocks, value_up, output_weight
):
    step_total, row_count, nope_all = query_nope.shape
    heads_local, nope_width, latent_width = key_up.shape
    rope_width = cache_rope.shape[1] // 2
    score_scale = (nope_width + rope_width) ** (-0.5)
    nope_rows = query_nope.reshape(step_total, row_count, heads_local, nope_width)
    query_latent = jnp.einsum(
        "srhn,hnl->srhl", nope_rows, key_up, preferred_element_type=jnp.float32
    ).astype(jnp.bfloat16)
    query_rot = query_rope.reshape(step_total, row_count, heads_local, rope_width)
    capacity = 3 * row_count * chosen_blocks.shape[2] // lax.axis_size("ctx")
    value_float = value_up.astype(jnp.float32)
    results = []
    for step_index in range(step_total):
        results.append(
            attend_rows(
                query_latent[step_index],
                query_rot[step_index],
                chosen_blocks[step_index],
                cache_latent,
                cache_rope,
                value_float,
                output_weight,
                capacity,
                1,
                score_scale,
            )
        )
    return jnp.concatenate(results, axis=0)


def solution(mesh):
    placed = (
        P(None, None, "head"),
        P(None, None, "head"),
        P("head", None, None),
        P("ctx", None),
        P("ctx", None),
        P(),
        P("head", "ctx", None),
        P("head", "ctx"),
    )
    return jax.shard_map(
        body, mesh=mesh, in_specs=placed, out_specs=P(None, "head", "ctx"), check_vma=False
    )
```

profile of v0, /device:TPU:6, one launch (start us, length us, event | category | flops | bytes accessed | tf_op | source)
XLA Modules:
  0.0 869.2 jit_solution(15680970266058695532)
XLA Ops:
  6.5 0.9 fusion.43
  7.8 3.8 sort.32
  11.6 3.8 sort.31
  15.4 0.7 gather_fusion.2
  16.8 0.7 gather_fusion.9
  18.3 1.2 reshape.244
  21.0 2.5 gather_fusion.3
  23.5 2.5 gather_fusion.10
  27.4 0.8 squeeze.20
  28.4 2.0 fusion.48
  30.6 1.1 copy.36
  31.7 2.2 gather_fusion.4
  34.0 2.5 gather_fusion.1
  36.4 1.1 copy.42
  37.5 1.3 gather_fusion.11
  38.8 1.7 gather_fusion.8
  40.6 3.0 fusion.46
  44.2 2.8 fusion.47
  47.0 1.2 fusion.44
  48.5 253.8 %all-reduce.4 = (f32[32,16]{1,0:T(8,128)S(1)}, f32[32,16]{1,0:T(8,128)S(1)}) all-reduce(f32[32,16]{1,0:T(8,128)S(1)} %copy.44, f32[32,16]{1,0:T(8,128)S(1)} %copy.38), channel_id=1, replica_groups=mesh['ctx'=64,'head'=4] {'ctx'}, use_global_device_ids=true, to_apply=%region_12.13 | all-reduce | flops 1024 | bytes 8192 | tf_op jit(solution)/shard_map/pmax | solution.py:63
  303.1 2.5 convolution_multiply_fusion.1
  305.6 5.0 fusion.4
  311.4 2.5 convolution_multiply_fusion
  313.9 5.0 fusion.2
  319.5 128.8 %reduce-scatter.5.cloned.1.call-done = f32[32,16,8]{0,2,1:T(8,128)} async-done(((f32[32,16,512]{0,2,1:T(8,128)}), f32[32,16,8]{0,2,1:T(8,128)}) %reduce-scatter.5.cloned.1.call-update) | async-done | bytes 16400 | tf_op jit(solution)/shard_map/reduce_scatter | solution.py:70
  448.3 1.9 convolution_bitcast_fusion.1
  450.3 145.0 %reduce-scatter.7.cloned.1.call-done = f32[32,16,8]{0,2,1:T(8,128)} async-done(((f32[32,16,512]{0,2,1:T(8,128)}), f32[32,16,8]{0,2,1:T(8,128)}) %reduce-scatter.7.cloned.1.call-update) | async-done | bytes 16400 | tf_op jit(solution)/shard_map/reduce_scatter | solution.py:70
  595.3 1.9 convolution_bitcast_fusion
  598.9 246.2 %all-reduce.2 = (f32[32,16]{0,1:T(8,128)S(1)}, f32[32,16]{0,1:T(8,128)S(1)}) all-reduce(f32[32,16]{0,1:T(8,128)S(1)} %fusion.20, f32[32,16]{0,1:T(8,128)S(1)} %fusion.22), channel_id=1, replica_groups=mesh['ctx'=64,'head'=4] {'ctx'}, use_global_device_ids=true, to_apply=%region_16.17 | all-reduce | flops 1024 | bytes 8192 | tf_op jit(solution)/shard_map/psum | solution.py:72
  845.1 1.4 convolution_bitcast_fusion.2
  846.5 1.4 convolution_bitcast_fusion.3
  847.9 14.1 %all-reduce.5 = (bf16[1,32,112]{2,1,0:T(8,128)(2,1)S(1)}, bf16[1,32,112]{2,1,0:T(8,128)(2,1)S(1)}) all-reduce(f32[1,32,112]{2,1,0:T(8,128)S(1)} %convolution_bitcast_fusion.2, f32[1,32,112]{2,1,0:T(8,128)S(1)} %convolution_bitcast_fusion.3), channel_id=5, replica_groups=mesh['ctx'=64,'head'=4] {'head'}, use_global_device_ids=true, to_apply=%region_17.18.clone | all-reduce | flops 7168 | bytes 43008
  (75 shorter events, 9.7 us)
Async XLA Ops:
  6.5 14.4 %copy-start = (bf16[2048,512]{1,0:T(8,128)(2,1)S(1)}, bf16[2048,512]{1,0:T(8,128)(2,1)}, u32[]{:S(2)}) copy-start(bf16[2048,512]{1,0:T(8,128)(2,1)} %param.11) | copy-start | bytes 6291460
  6.5 441.8 %reduce-scatter.5.cloned.1.call-start = ((), (), s32[]{:S(2)}) async-start(), calls=%async_computation.2 | async-start | bytes 4259840 | tf_op jit(solution)/shard_map/reduce_scatter | solution.py:70
  11.5 15.7 %copy-start.7 = (s32[24]{0:T(128)}, s32[24]{0:T(128)S(1)}, u32[]{:S(2)}) copy-start(s32[24]{0:T(128)S(1)} %get-tuple-element.22) | copy-start | bytes 292
  15.3 11.9 %copy-start.5 = (s32[24]{0:T(128)}, s32[24]{0:T(128)S(1)}, u32[]{:S(2)}) copy-start(s32[24]{0:T(128)S(1)} %get-tuple-element.18) | copy-start | bytes 292
  23.5 3.9 copy-start.3
  23.5 4.8 copy-start.2
  40.6 3.0 copy-start.1
  47.0 258.6 %copy-start.6 = (s32[24]{0:T(128)S(1)}, s32[24]{0:T(128)}, u32[]{:S(2)}) copy-start(s32[24]{0:T(128)} %copy-done.5) | copy-start | bytes 292
  310.6 3.3 copy-start.8
  310.6 284.6 %reduce-scatter.7.cloned.1.call-start = ((), (), s32[]{:S(2)}) async-start(), calls=%async_computation.3 | async-start | bytes 4259840 | tf_op jit(solution)/shard_map/reduce_scatter | solution.py:70
  318.9 129.4 %copy-start.4 = (bf16[16,8,128]{2,1,0:T(8,128)(2,1)S(1)}, bf16[16,8,128]{2,1,0:T(8,128)(2,1)}, u32[]{:S(2)}) copy-start(bf16[16,8,128]{2,1,0:T(8,128)(2,1)} %param.14) | copy-start | bytes 98308
  318.9 278.5 %copy-start.9 = (u32[256]{0:T(256)S(1)}, u32[256]{0:T(256)}, u32[]{:S(2)}) copy-start(u32[256]{0:T(256)} %constant.66) | copy-start | bytes 3076
  319.0 526.2 %all-reduce.8.cloned.1.call-start = ((), (), s32[]{:S(2)}) async-start(), calls=%async_computation.4 | async-start | bytes 1048576 | tf_op jit(solution)/shard_map/psum | solution.py:72
Sparse Core Ops, SparseCore 0:
  310.7 137.5 reduce-scatter.4
  453.0 142.2 reduce-scatter.6
  598.8 179.7 all-reduce.7
where the time goes:
time: 871 us; the launch traced here: 869 us
  blocking collectives  514 us (59%)
  waiting for transfers between devices  274 us (31%)
  matrix products  31.3 us (4%)
  local copies, waits for them, and re-layouts  24.9 us (3%)
  between operations  14.1 us (2%)
  other arithmetic  10.7 us (1%)
    reduce_scatter x2, waiting for transfers between devices, attend_rows(): own_share = lax.psum_scatter(merged, 'ctx', scatter_dimension=2, tiled=True)  274 us
    pmax x1, blocking collectives, attend_rows(): row_top = lax.pmax(local_peak, 'ctx')  254 us
    psum x1, blocking collectives, attend_rows(): head_sum, row_total = lax.psum((partial_value, row_total), 'ctx')  246 us
  transfers between devices with their start and end apart: 3, of which 2 were waited for; matrix products, arithmetic and copies ran while one was open for 1% of the time, Pallas kernels for 0%

commit v1 on v0

v1 whole, which is shorter than its diff:
```python
import functools

import jax
import jax.numpy as jnp
from jax import lax
from jax.experimental import pallas as pl
from jax.experimental.pallas import tpu as pltpu
from jax.sharding import Mesh
from jax.sharding import PartitionSpec as P

BLOCK = 128
LATENT = 512
HEADS = 16
ROWS = 32
ITEMS = HEADS * ROWS
ROW_STRIDE = 40
HEAD_STRIDE = 24
LANES = 128
UNROLL = 16
EARLY_ROWS = 8
PER_STEP = 16
PAIRS = 48
NONE = -1e30
MASKED = -3e38
F32 = jnp.float32
BF16 = jnp.bfloat16


def dot_t(a, b):
    return lax.dot_general(a, b, (((1,), (1,)), ((), ())), preferred_element_type=F32)


def dot(a, b):
    return jnp.dot(a, b, preferred_element_type=F32)


def split3(x):
    hi = x.astype(BF16).astype(F32)
    mid = (x - hi).astype(BF16).astype(F32)
    return hi, mid, x - hi - mid


def pack_stats(peak, total):
    lane = lax.broadcasted_iota(jnp.int32, peak.shape, 1) // 16
    parts = split3(peak) + split3(total)
    out = parts[0]
    for i in range(1, 6):
        out = jnp.where(lane == i, parts[i], out)
    return out.astype(BF16)


def spread_stats(packed, lanes_each):
    part = lax.broadcasted_iota(jnp.int32, (LANES, 2 * LANES), 0)
    side = lax.broadcasted_iota(jnp.int32, (LANES, 2 * LANES), 1) // LANES
    used = (part % 16 < lanes_each) & (part // 48 == side) & (part < 96)
    both = dot(packed, used.astype(BF16))
    return both[:, :LANES], both[:, LANES:]


def own_lanes(stats):
    lane = lax.broadcasted_iota(jnp.int32, stats.shape, 2) % 16
    return jnp.where(lane == lax.broadcasted_iota(jnp.int32, stats.shape, 1), stats, 0.0)


def attend_kernel(
    chosen_hbm, q_nope_hbm, q_rope_hbm, value_hbm, key_hbm, latent_hbm, rope_hbm, keep, send,
    chosen, acc, peak, total, q_nope, q_rope, key, latent, rope, q_lat, q_rot, rope_wide, scores, pairs, sems, *, scale
):
    core = lax.axis_index("core")
    device = (lax.axis_index("y") * 8 + lax.axis_index("z")) * 2 + core
    n_rows = 2 * ROWS
    copies = [
        pltpu.make_async_copy(src, dst, sems.at[i])
        for i, (src, dst) in enumerate(
            (
                (chosen_hbm, chosen),
                (q_nope_hbm, q_nope),
                (q_rope_hbm, q_rope),
                (rope_hbm, rope),
                (key_hbm, key),
                (latent_hbm, latent),
                (value_hbm, send.at[pl.ds(5 * ITEMS, LANES)]),
            )
        )
    ]
    for copy in copies:
        copy.start()

    copies[0].wait()

    def find(r, count):
        for s in range(2):
            offset = ((s ^ core) * ROWS + r) * 16 - device * 16
            for k in range(16):
                block = chosen[s, k, r]
                pairs[count] = block + offset
                count = count + ((block >> 4) == device).astype(jnp.int32)
        return count

    count = lax.fori_loop(0, EARLY_ROWS, find, jnp.int32(0))

    tok = lax.broadcasted_iota(jnp.int32, (BLOCK, BLOCK // 2), 0)
    pair = lax.broadcasted_iota(jnp.int32, (BLOCK, BLOCK // 2), 1)
    spread = (tok // 2 == pair).astype(BF16)
    half = (
        lax.broadcasted_iota(jnp.int32, (BLOCK, LANES), 1) // (LANES // 2)
        == lax.broadcasted_iota(jnp.int32, (BLOCK, LANES), 0) % 2
    )
    low = lax.broadcasted_iota(jnp.int32, (n_rows, LANES), 1) < LANES // 2

    late = (ROWS - EARLY_ROWS) * PER_STEP // HEADS

    def prepare(i, count):
        for u in range(late):
            count = find(EARLY_ROWS + i * late + u, count)
        for u in range(PER_STEP // 2):
            g = i * (PER_STEP // 2) + u
            two = q_rope[:, pl.ds(pl.multiple_of(g * LANES, LANES), LANES)].astype(F32)
            turned = pltpu.roll(two, LANES // 2, 1)
            q_rot[pl.ds(2 * g, n_rows, stride=HEAD_STRIDE), :] = jnp.where(low, two, turned)
            q_rot[pl.ds(2 * g + 1, n_rows, stride=HEAD_STRIDE), :] = jnp.where(low, turned, two)
        for u in range(PER_STEP):
            h = PER_STEP * i + u
            nope = q_nope[:, pl.ds(pl.multiple_of(h * LANES, LANES), LANES)]
            wide = dot(nope, key[h])
            for j in range(4):
                q_lat[j, pl.ds(h, n_rows, stride=HEAD_STRIDE), :] = wide[:, j * LANES : (j + 1) * LANES]
            keys = rope[pl.ds(pl.multiple_of(h * 64, 64), 64), :]
            there = pl.ds(pl.multiple_of(h * BLOCK, BLOCK), BLOCK)
            rope_wide[there, :] = jnp.where(half, dot(spread, keys), 0.0).astype(BF16)
        span = 2 * PER_STEP * ROW_STRIDE
        part = pl.ds(pl.multiple_of(i * span, span), span)
        for j in range(4):
            acc[j, part, :] = jnp.zeros((span, LANES), F32)
        total[part, :] = jnp.zeros((span, LANES), F32)
        peak[part, :] = jnp.full((span, LANES), NONE, F32)
        return count

    for copy in copies[1:5]:
        copy.wait()
    count = lax.fori_loop(0, HEADS // PER_STEP, prepare, count)
    for i in range(UNROLL):
        pairs[count + i] = 0
    chunks = (count + UNROLL - 1) // UNROLL
    copies[5].wait()

    def place(code):
        rel = code >> 4
        rel_step = rel >> 5
        row = rel & (ROWS - 1)
        first = pl.multiple_of(((rel_step ^ core) * ROWS + row) * HEAD_STRIDE, 8)
        where = pl.ds(rel_step * (HEADS * ROW_STRIDE) + row, HEADS, stride=ROW_STRIDE)
        tokens = pl.ds(pl.multiple_of((code & 15) * BLOCK, BLOCK), BLOCK)
        return pl.ds(first, HEADS), where, tokens

    def score(c, _):
        for u in range(UNROLL):
            p = c * UNROLL + u
            heads, where, tokens = place(pairs[p])
            query = jnp.concatenate([q_lat[j, heads, :] for j in range(4)], axis=1).astype(BF16)
            s = dot_t(latent[tokens, :], query) + dot_t(
                rope_wide[tokens, :], q_rot[heads, :].astype(BF16)
            )
            s = jnp.where(p < count, s.T * scale, MASKED)
            scores[p] = s
            peak[where, :] = jnp.maximum(peak[where, :], s)
        return 0

    lax.fori_loop(0, chunks, score, 0)
    for i in range(2 * HEADS):
        part = pl.ds(i * ROW_STRIDE, ROWS)
        peak[part, :] = jnp.broadcast_to(jnp.max(peak[part, :], axis=1, keepdims=True), (ROWS, LANES))

    def weigh(c, _):
        for u in range(UNROLL):
            p = c * UNROLL + u
            _, where, tokens = place(pairs[p])
            shifted = jnp.exp(scores[p] - peak[where, :])
            total[where, :] += shifted
            out = dot(shifted.astype(BF16), latent[tokens, :])
            for j in range(4):
                acc[j, where, :] += out[:, j * LANES : (j + 1) * LANES]
        return 0

    lax.fori_loop(0, chunks, weigh, 0)
    for i in range(2 * HEADS):
        part = pl.ds(i * ROW_STRIDE, ROWS)
        sums = jnp.broadcast_to(jnp.sum(total[part, :], axis=1, keepdims=True), (ROWS, LANES))
        there = [pl.ds(j * ITEMS + (i % HEADS) * ROWS, ROWS) for j in range(6)]
        if i < HEADS:
            for j in range(4):
                keep[there[j], :] = acc[j, part, :]
            keep[there[4], :] = peak[part, :]
            keep[there[5], :] = sums
        else:
            for j in range(4):
                send[there[j], :] = acc[j, part, :].astype(BF16)
            send[there[4], :] = pack_stats(peak[part, :], sums)
    copies[6].wait()


def gather_lanes(stats, copies):
    n = stats.shape[0] // 16
    kept = own_lanes(stats.astype(F32).reshape(n, 16, LANES)).reshape(n * 16, LANES).astype(BF16)
    row = lax.broadcasted_iota(jnp.int32, (n * copies, n * 16), 0) // copies
    item = lax.broadcasted_iota(jnp.int32, (n * copies, n * 16), 1) // 16
    return dot((row == item).astype(BF16), kept).astype(BF16)


def pair_kernel(keep, got, value, out0, out1, out2, out3, f1, f2, stats):
    core = lax.axis_index("core")
    me = lax.axis_index("y")
    n = 16
    m2, l2 = spread_stats(got[4 * ITEMS : 5 * ITEMS, :], 1)
    m1, l1 = keep[4 * ITEMS : 5 * ITEMS, :], keep[5 * ITEMS :, :]
    top = jnp.maximum(m1, m2)
    f1[...] = jnp.exp(m1 - top)
    f2[...] = jnp.exp(m2 - top)
    stats[...] = gather_lanes(pack_stats(top, l1 * f1[...] + l2 * f2[...]), 2).astype(F32)
    for k, out in enumerate((out0, out1, out2, out3)):
        to = (me + k) & 3
        for g in range(8):
            a = pl.ds(pl.multiple_of(to * 128 + g * n, n), n)
            for j in range(4):
                here = pl.ds(pl.multiple_of(j * ITEMS + to * 128 + g * n, n), n)
                both = keep[here, :] * f1[a, :] + got[here, :].astype(F32) * f2[a, :]
                out[g * 64 + j * n : g * 64 + (j + 1) * n, :] = both.astype(BF16)
        for i in range(2):
            own = value[pl.ds(pl.multiple_of(to * 32 + i * n, n), n), :].astype(F32)
            sib = got[pl.ds(pl.multiple_of(5 * ITEMS + to * 32 + i * n, n), n), :].astype(F32)
            first = jnp.where(core == 0, own, sib)
            second = jnp.where(core == 0, sib, own)
            for u in range(2):
                rows = slice(u * 8, u * 8 + 8)
                piece = jnp.concatenate([first[rows], second[rows]], axis=0).astype(BF16)
                at = 512 + (2 * i + u) * n
                out[at : at + n, :] = piece
        out[576:592, :] = stats[pl.ds(pl.multiple_of(to * 16, 16), 16), :].astype(BF16)


def cross_kernel(own, got1, got2, got3, out):
    me = lax.axis_index("y")
    n = 16
    sources = (own, got1, got2, got3)
    packed = []
    for src in sources:
        rows = src[576:592, :].astype(F32).reshape(8, 2, LANES)[:, :1]
        packed.append(own_lanes(jnp.broadcast_to(rows, (8, n, LANES))).reshape(128, LANES))
    tops, sums = spread_stats(jnp.concatenate(packed, axis=0).astype(BF16), n)
    tops, sums = tops.reshape(4, 128, LANES), sums.reshape(4, 128, LANES)
    top = jnp.max(tops, axis=0)
    factors = jnp.exp(tops - top[None])
    stats = pack_stats(top, jnp.sum(factors * sums, axis=0))
    out[:, 128:136, :] = gather_lanes(stats, 8).reshape(8, 8, LANES)
    for g in range(8):
        for j in range(4):
            here = slice(g * 64 + j * n, g * 64 + (j + 1) * n)
            total = jnp.zeros((n, LANES), F32)
            for k, src in enumerate(sources):
                total += src[here, :].astype(F32) * factors[k, g * n : (g + 1) * n]
            out[g, j * n : (j + 1) * n, :] = total.astype(BF16)
        for k, src in enumerate(sources):
            origin = (me + 4 - k) & 3
            at = 512 + (g // 2) * n
            out[g, pl.ds(pl.multiple_of(64 + origin * n, n), n), :] = src[at : at + n, :]


def merge_kernel(got, out):
    packed = got[:, 128:136, :].astype(F32)
    packed = own_lanes(jnp.concatenate([packed, packed], axis=1)).astype(BF16)
    tops, sums = (x.reshape(8, 16, LANES) for x in spread_stats(packed.reshape(128, LANES), 16))
    factors = jnp.exp(tops - jnp.max(tops, axis=0, keepdims=True))
    total = jnp.sum(factors * sums, axis=0)
    result = jnp.zeros((16, LANES), F32)
    for j in range(4):
        merged = jnp.sum(got[:, j * 16 : (j + 1) * 16, :].astype(F32) * factors, axis=0)
        value = got[:, 64 + j * 16 : 80 + j * 16, :].reshape(128, LANES)
        for part in split3(merged):
            result += dot(part.astype(BF16), value)
    result = (result / total).astype(BF16)
    for s in range(32):
        out[s] = result


def project_kernel(own, sib, weight, *outs):
    core = lax.axis_index("core")
    me = lax.axis_index("head")
    zero = core == 0
    total = jnp.zeros((2 * ROWS, weight.shape[0]), F32)
    for h in range(HEADS):
        mine = own[2 * h : 2 * h + 2].reshape(ROWS, LANES)
        other = sib[2 * h : 2 * h + 2].reshape(ROWS, LANES)
        rows = jnp.concatenate([jnp.where(zero, mine, other), jnp.where(zero, other, mine)], axis=0)
        total += dot_t(rows, weight[:, h * LANES : (h + 1) * LANES])
    total = total.reshape(2, 4, 8, weight.shape[0])
    for k in range(4):
        want = lax.rem(me + k, 4)
        part = total[:, 0]
        for i in range(1, 4):
            part = jnp.where(want == i, total[:, i], part)
        outs[k][...] = part


VMEM = pl.BlockSpec(memory_space=pltpu.VMEM)
SMEM = pl.BlockSpec(memory_space=pltpu.SMEM)
HBM = pl.BlockSpec(memory_space=pltpu.HBM)


def params(mebibytes=8):
    return pltpu.CompilerParams(vmem_limit_bytes=mebibytes * 1024 * 1024)


def body(
    query_nope, query_rope, key_up, cache_latent, cache_rope, chosen_blocks, value_up, output_weight
):
    steps, rows, _ = query_nope.shape
    heads, nope, latent = key_up.shape
    rot = cache_rope.shape[1] // 2
    scale = (nope + rot) ** (-0.5)
    swap = [(0, 1), (1, 0)]
    value = value_up.reshape(-1, LANES)
    n_rows = steps * rows
    keep, send = pl.pallas_call(
        functools.partial(attend_kernel, scale=scale),
        out_shape=(
            jax.ShapeDtypeStruct((6 * ITEMS, LANES), F32),
            jax.ShapeDtypeStruct((5 * ITEMS + value.shape[0], LANES), BF16),
        ),
        in_specs=[HBM] * 7,
        out_specs=(VMEM,) * 2,
        scratch_shapes=[
            pltpu.SMEM((steps, chosen_blocks.shape[2], rows), jnp.int32),
            pltpu.VMEM((4, steps * heads * ROW_STRIDE, LANES), F32),
            pltpu.VMEM((steps * heads * ROW_STRIDE, LANES), F32),
            pltpu.VMEM((steps * heads * ROW_STRIDE, LANES), F32),
            pltpu.VMEM((n_rows, heads * nope), BF16),
            pltpu.VMEM((n_rows, heads * rot), BF16),
            pltpu.VMEM(key_up.shape, BF16),
            pltpu.VMEM(cache_latent.shape, BF16),
            pltpu.VMEM(cache_rope.shape, BF16),
            pltpu.VMEM((4, n_rows * HEAD_STRIDE, LANES), F32),
            pltpu.VMEM((n_rows * HEAD_STRIDE, LANES), F32),
            pltpu.VMEM((cache_latent.shape[0], LANES), BF16),
            pltpu.VMEM((PAIRS + UNROLL, HEADS, LANES), F32),
            pltpu.SMEM((PAIRS + UNROLL,), jnp.int32),
            pltpu.SemaphoreType.DMA((7,)),
        ],
        compiler_params=params(40),
        name="attend",
    )(
        *(
            pltpu.with_memory_space_constraint(x, pltpu.HBM)
            for x in (
                chosen_blocks.transpose(0, 2, 1),
                query_nope.reshape(n_rows, -1),
                query_rope.reshape(n_rows, -1),
                value,
                key_up,
                cache_latent,
                cache_rope,
            )
        ),
    )
    got = lax.ppermute(send, "core", swap)
    blocks = pl.pallas_call(
        pair_kernel,
        out_shape=(jax.ShapeDtypeStruct((592, LANES), BF16),) * 4,
        in_specs=[VMEM] * 3,
        out_specs=(VMEM,) * 4,
        scratch_shapes=[
            pltpu.VMEM((ITEMS, LANES), F32),
            pltpu.VMEM((ITEMS, LANES), F32),
            pltpu.VMEM((64, LANES), F32),
        ],
        compiler_params=params(),
        name="pair",
    )(keep, got, value)
    got = [
        lax.ppermute(blocks[k], "y", [(i, (i + k) % 4) for i in range(4)]) for k in range(1, 4)
    ]
    packed = pl.pallas_call(
        cross_kernel,
        out_shape=jax.ShapeDtypeStruct((8, 136, LANES), BF16),
        in_specs=[VMEM] * 4,
        out_specs=VMEM,
        compiler_params=params(),
        name="cross",
    )(blocks[0], *got)
    parts = lax.all_to_all(packed, "z", 0, 0)
    values = pl.pallas_call(
        merge_kernel,
        out_shape=jax.ShapeDtypeStruct((32, 16, LANES), BF16),
        in_specs=[VMEM],
        out_specs=VMEM,
        compiler_params=params(),
        name="merge",
    )(parts)
    own = lax.all_to_all(values, ("y", "z"), 0, 0)
    sib = lax.ppermute(own, "core", swap)
    width = output_weight.shape[1]
    terms = pl.pallas_call(
        project_kernel,
        out_shape=(jax.ShapeDtypeStruct((steps, rows // 4, width), F32),) * 4,
        in_specs=[VMEM] * 3,
        out_specs=(VMEM,) * 4,
        compiler_params=params(),
        name="project",
    )(own, sib, output_weight.transpose(1, 0))
    out = terms[0]
    for k in range(1, 4):
        out = out + lax.ppermute(terms[k], "head", [(i, (i + k) % 4) for i in range(4)])
    return out.astype(BF16)


def solution(mesh):
    fine = Mesh(mesh.devices.reshape(4, 8, 2, 4), ("y", "z", "core", "head"))
    ctx = ("y", "z", "core")
    placed = (
        P(None, None, "head"),
        P(None, None, "head"),
        P("head", None, None),
        P(ctx, None),
        P(ctx, None),
        P(),
        P("head", ctx, None),
        P("head", ctx),
    )
    return jax.shard_map(
        body, mesh=fine, in_specs=placed, out_specs=P(None, "head", ctx), check_vma=False
    )
```

time: 871 us -> 67.6 us (0.08)
  blocking collectives: 514 us -> 33.9 us
  waiting for transfers between devices: 274 us -> 13.2 us
  matrix products: 31.3 us -> 0 us
  local copies, waits for them, and re-layouts: 24.9 us -> 0.01 us
  between operations: 14.1 us -> 0.04 us
  starting transfers between devices: 0.09 us -> 11.6 us
  other arithmetic: 10.7 us -> 0.6 us
    reduce_scatter x2 -> x0, waiting for transfers between devices: 274 us -> none  [attend_rows(): own_share = lax.psum_scatter(merged, 'ctx', scatter_dimension=2, tiled=True)]
    pmax x1 -> x0, blocking collectives: 254 us -> none  [attend_rows(): row_top = lax.pmax(local_peak, 'ctx')]
    psum x1 -> x0, blocking collectives: 246 us -> none  [attend_rows(): head_sum, row_total = lax.psum((partial_value, row_total), 'ctx')]
    all_to_all x0 -> x2, blocking collectives: none -> 33.9 us  [the longest x1 19.2 us: body(): parts = lax.all_to_all(packed, 'z', 0, 0)]
    dot_general x14 -> x0, matrix products: 29.3 us -> none  [the longest x2 10.1 us: attend_rows(): jnp.einsum('rp,phl->rhl', member_float, factor[..., None] * block_out, pr...]
    gather x14 -> x0, local copies, waits for them, and re-layouts: 18.3 us -> none  [the longest x2 5.04 us: attend_rows(): cache_latent.reshape(blocks_here, BLOCK, latent_width)[pair_block]]
    unnamed x1 -> x0, blocking collectives: 14.1 us -> none
    ppermute x0 -> x8, waiting for transfers between devices: none -> 13.2 us  [the longest x3 4.86 us: body(): lax.ppermute(terms[k], 'head', [(i, (i + k) % 4) for i in range(4)])]
  transfers between devices with their start and end apart: 3 -> 8, of which waited for: 2 -> 6; matrix products, arithmetic and copies ran while one was open for 1% -> 0% of each run, Pallas kernels for 0% -> 0%
where the time goes in v1:
time: 67.6 us; the launch traced here: 67.5 us
  blocking collectives  33.9 us (50%)
  waiting for transfers between devices  13.2 us (20%)
  starting transfers between devices  11.6 us (17%)
  Pallas kernels  8.15 us (12%)
    all_to_all x1, blocking collectives, body(): parts = lax.all_to_all(packed, 'z', 0, 0)  19.2 us
    all_to_all x1, blocking collectives, body(): own = lax.all_to_all(values, ('y', 'z'), 0, 0)  14.7 us
    ppermute x3, starting transfers between devices, body(): lax.ppermute(blocks[k], 'y', [(i, (i + k) % 4) for i in range(4)])  8.55 us
    pallas_call x1, Pallas kernels, body(): pl.pallas_call(functools.partial(attend_kernel, scale=scale), out_shape=(...  6.03 us
    ppermute x3, waiting for transfers between devices, body(): lax.ppermute(terms[k], 'head', [(i, (i + k) % 4) for i in range(4)])  4.86 us
    ppermute x3, waiting for transfers between devices, body(): lax.ppermute(blocks[k], 'y', [(i, (i + k) % 4) for i in range(4)])  4.85 us
    ppermute x3, starting transfers between devices, body(): lax.ppermute(terms[k], 'head', [(i, (i + k) % 4) for i in range(4)])  2.96 us
    ppermute x1, waiting for transfers between devices, body(): got = lax.ppermute(send, 'core', swap)  2.13 us
  transfers between devices with their start and end apart: 8, of which 6 were waited for; matrix products, arithmetic and copies ran while one was open for 0% of the time, Pallas kernels for 0%

profile of v1, /device:TPU:6, one launch (start us, length us, event | category | flops | bytes accessed | tf_op | source)
XLA Modules:
  0.0 67.5 jit_solution(12236127056164935528)
XLA Ops:
  0.0 0.0 copy-start.1
  0.0 6.0 %attend.1 = (f32[3072,128]{1,0:T(8,128)S(1)}, bf16[2688,128]{1,0:T(8,128)(2,1)S(1)}) custom-call(s32[2,16,32]{2,1,0:T(8,128)} %bitcast.10, bf16[64,2048]{1,0:T(8,128)(2,1)} %bitcast.8, bf16[64,1024]{1,0:T(8,128)(2,1)} %bitcast.9, bf16[128,128]{1,0:T(8,128)(2,1)} %bitcast.6, bf16[16,128,512]{2,1,0:T(8,128)(2,1)} %key_hbm.1, bf16[2048,512]{1,0:T(8,128)(2,1)} %latent_hbm.1, ...), custom_call_target="tpu_custom_call" | custom-call | tf_op jit(solution)/shard_map/attend/pallas_call | solution.py:323
  6.0 0.1 collective-permute-start
  6.1 2.1 %collective-permute-done.got = bf16[2688,128]{1,0:T(8,128)(2,1)S(1)} collective-permute-done((bf16[2688,128]{1,0:T(8,128)(2,1)S(1)}, bf16[2688,128]{1,0:T(8,128)(2,1)S(1)}, u32[]{:S(2)}, u32[]{:S(2)}) %collective-permute-start) | collective-permute-done | bytes 688160 | tf_op jit(solution)/shard_map/ppermute | solution.py:364
  8.3 0.0 copy-done.1
  8.3 0.0 copy-start
  8.3 0.8 %pair.1 = (bf16[592,128]{1,0:T(8,128)(2,1)S(1)}, bf16[592,128]{1,0:T(8,128)(2,1)S(1)}, bf16[592,128]{1,0:T(8,128)(2,1)S(1)}, bf16[592,128]{1,0:T(8,128)(2,1)S(1)}) custom-call(f32[3072,128]{1,0:T(8,128)S(1)} %get-tuple-element.15.keep, bf16[2688,128]{1,0:T(8,128)(2,1)S(1)} %collective-permute-done.got, bf16[128,128]{1,0:T(8,128)(2,1)S(1)} %bitcast.7), custom_call_target="tpu_custom_call" | custom-call | tf_op jit(solution)/shard_map/pair/pallas_call | solution.py:365
  9.1 1.7 %collective-permute-start.1 = (bf16[592,128]{1,0:T(8,128)(2,1)S(1)}, bf16[592,128]{1,0:T(8,128)(2,1)S(1)}, u32[]{:S(2)}, u32[]{:S(2)}) collective-permute-start(bf16[592,128]{1,0:T(8,128)(2,1)S(1)} %get-tuple-element.18), channel_id=1, source_target_pairs={{0,64},{64,128},{128,192},{192,0},{1,65},{65,129},{129,193},{193,1... | collective-permute-start | bytes 454664 | tf_op jit(solution)/shard_map/ppermute | solution.py:379
  10.7 4.4 %collective-permute-start.2 = (bf16[592,128]{1,0:T(8,128)(2,1)S(1)}, bf16[592,128]{1,0:T(8,128)(2,1)S(1)}, u32[]{:S(2)}, u32[]{:S(2)}) collective-permute-start(bf16[592,128]{1,0:T(8,128)(2,1)S(1)} %get-tuple-element.19), channel_id=1, source_target_pairs={{0,128},{64,192},{128,0},{192,64},{1,129},{65,193},{129,1},{193,65... | collective-permute-start | bytes 454664 | tf_op jit(solution)/shard_map/ppermute | solution.py:379
  15.1 2.5 %collective-permute-start.3 = (bf16[592,128]{1,0:T(8,128)(2,1)S(1)}, bf16[592,128]{1,0:T(8,128)(2,1)S(1)}, u32[]{:S(2)}, u32[]{:S(2)}) collective-permute-start(bf16[592,128]{1,0:T(8,128)(2,1)S(1)} %get-tuple-element.20), channel_id=1, source_target_pairs={{0,192},{64,0},{128,64},{192,128},{1,193},{65,1},{129,65},{193,129... | collective-permute-start | bytes 454664 | tf_op jit(solution)/shard_map/ppermute | solution.py:379
  17.6 0.0 collective-permute-done.1.got1
  17.6 4.8 %collective-permute-done.2.got2 = bf16[592,128]{1,0:T(8,128)(2,1)S(1)} collective-permute-done((bf16[592,128]{1,0:T(8,128)(2,1)S(1)}, bf16[592,128]{1,0:T(8,128)(2,1)S(1)}, u32[]{:S(2)}, u32[]{:S(2)}) %collective-permute-start.2) | collective-permute-done | bytes 151584 | tf_op jit(solution)/shard_map/ppermute | solution.py:379
  22.5 0.0 collective-permute-done.3.got3
  22.5 0.5 cross.1
  23.0 19.2 %all_to_all.10.got = bf16[8,136,128]{2,1,0:T(8,128)(2,1)S(1)} all-to-all(bf16[8,136,128]{2,1,0:T(8,128)(2,1)S(1)} %cross.1), channel_id=1, replica_groups=mesh['y'=4,'z'=8,'core'=2,'head'=4] {'z'}, dimensions={0} | all-to-all | bytes 557056 | tf_op jit(solution)/shard_map/all_to_all | solution.py:389
  42.2 0.4 merge.1
  42.6 14.7 %all_to_all.11.own = bf16[32,16,128]{2,1,0:T(8,128)(2,1)S(1)} all-to-all(bf16[32,16,128]{2,1,0:T(8,128)(2,1)S(1)} %merge.1), channel_id=1, replica_groups=mesh['y'=4,'z'=8,'core'=2,'head'=4] {'y','z'}, dimensions={0} | all-to-all | bytes 262144 | tf_op jit(solution)/shard_map/all_to_all | solution.py:398
  57.3 0.0 collective-permute-start.4
  57.3 1.3 %collective-permute-done.4.sib = bf16[32,16,128]{2,1,0:T(8,128)(2,1)S(1)} collective-permute-done((bf16[32,16,128]{2,1,0:T(8,128)(2,1)S(1)}, bf16[32,16,128]{2,1,0:T(8,128)(2,1)S(1)}, u32[]{:S(2)}, u32[]{:S(2)}) %collective-permute-start.4) | collective-permute-done | bytes 131104 | tf_op jit(solution)/shard_map/ppermute | solution.py:399
  58.6 0.0 copy-done
  58.7 0.4 project.1
  59.0 0.5 collective-permute-start.5
  59.6 2.4 %collective-permute-start.6 = (f32[2,8,112]{2,1,0:T(8,128)S(1)}, f32[2,8,112]{2,1,0:T(8,128)S(1)}, u32[]{:S(2)}, u32[]{:S(2)}) collective-permute-start(f32[2,8,112]{2,1,0:T(8,128)S(1)} %get-tuple-element.23), channel_id=1, source_target_pairs={{0,2},{1,3},{2,0},{3,1},{4,6},{5,7},{6,4},{7,5},{8,10},{9,11},{10,... | collective-permute-start | bytes 21512 | tf_op jit(solution)/shard_map/ppermute | solution.py:411
  62.0 0.0 collective-permute-start.7
  62.0 0.8 %collective-permute-done.5 = f32[2,8,112]{2,1,0:T(8,128)S(1)} collective-permute-done((f32[2,8,112]{2,1,0:T(8,128)S(1)}, f32[2,8,112]{2,1,0:T(8,128)S(1)}, u32[]{:S(2)}, u32[]{:S(2)}) %collective-permute-start.5) | collective-permute-done | bytes 7200 | tf_op jit(solution)/shard_map/ppermute | solution.py:411
  62.8 2.0 %collective-permute-done.6 = f32[2,8,112]{2,1,0:T(8,128)S(1)} collective-permute-done((f32[2,8,112]{2,1,0:T(8,128)S(1)}, f32[2,8,112]{2,1,0:T(8,128)S(1)}, u32[]{:S(2)}, u32[]{:S(2)}) %collective-permute-start.6) | collective-permute-done | bytes 7200 | tf_op jit(solution)/shard_map/ppermute | solution.py:411
  64.8 2.1 %collective-permute-done.7 = f32[2,8,112]{2,1,0:T(8,128)S(1)} collective-permute-done((f32[2,8,112]{2,1,0:T(8,128)S(1)}, f32[2,8,112]{2,1,0:T(8,128)S(1)}, u32[]{:S(2)}, u32[]{:S(2)}) %collective-permute-start.7) | collective-permute-done | bytes 7200 | tf_op jit(solution)/shard_map/ppermute | solution.py:411
  66.9 0.6 add_convert_fusion
Async XLA Ops:
  0.0 8.3 %copy-start.1 = (bf16[16,8,128]{2,1,0:T(8,128)(2,1)S(1)}, bf16[16,8,128]{2,1,0:T(8,128)(2,1)}, u32[]{:S(2)}) copy-start(bf16[16,8,128]{2,1,0:T(8,128)(2,1)} %param.14) | copy-start | bytes 98308
  6.0 2.2 %collective-permute-start = (bf16[2688,128]{1,0:T(8,128)(2,1)S(1)}, bf16[2688,128]{1,0:T(8,128)(2,1)S(1)}, u32[]{:S(2)}, u32[]{:S(2)}) collective-permute-start(bf16[2688,128]{1,0:T(8,128)(2,1)S(1)} %get-tuple-element.16), channel_id=1, source_target_pairs={{0,4},{4,0},{1,5},{5,1},{2,6},{6,2},{3,7},{7,3},{8,12},{12,8},{9,1... | collective-permute-start | bytes 2064392 | tf_op jit(solution)/shard_map/ppermute | solution.py:364
  8.3 50.4 %copy-start = (bf16[2048,112]{0,1:T(8,128)(2,1)S(1)}, bf16[2048,112]{0,1:T(8,128)(2,1)}, u32[]{:S(2)}) copy-start(bf16[2048,112]{0,1:T(8,128)(2,1)} %param.15) | copy-start | bytes 1376260
  9.1 8.6 %collective-permute-start.1 = (bf16[592,128]{1,0:T(8,128)(2,1)S(1)}, bf16[592,128]{1,0:T(8,128)(2,1)S(1)}, u32[]{:S(2)}, u32[]{:S(2)}) collective-permute-start(bf16[592,128]{1,0:T(8,128)(2,1)S(1)} %get-tuple-element.18), channel_id=1, source_target_pairs={{0,64},{64,128},{128,192},{192,0},{1,65},{65,129},{129,193},{193,1... | collective-permute-start | bytes 454664 | tf_op jit(solution)/shard_map/ppermute | solution.py:379
  10.7 11.8 %collective-permute-start.2 = (bf16[592,128]{1,0:T(8,128)(2,1)S(1)}, bf16[592,128]{1,0:T(8,128)(2,1)S(1)}, u32[]{:S(2)}, u32[]{:S(2)}) collective-permute-start(bf16[592,128]{1,0:T(8,128)(2,1)S(1)} %get-tuple-element.19), channel_id=1, source_target_pairs={{0,128},{64,192},{128,0},{192,64},{1,129},{65,193},{129,1},{193,65... | collective-permute-start | bytes 454664 | tf_op jit(solution)/shard_map/ppermute | solution.py:379
  15.1 7.4 %collective-permute-start.3 = (bf16[592,128]{1,0:T(8,128)(2,1)S(1)}, bf16[592,128]{1,0:T(8,128)(2,1)S(1)}, u32[]{:S(2)}, u32[]{:S(2)}) collective-permute-start(bf16[592,128]{1,0:T(8,128)(2,1)S(1)} %get-tuple-element.20), channel_id=1, source_target_pairs={{0,192},{64,0},{128,64},{192,128},{1,193},{65,1},{129,65},{193,129... | collective-permute-start | bytes 454664 | tf_op jit(solution)/shard_map/ppermute | solution.py:379
  57.3 1.3 %collective-permute-start.4 = (bf16[32,16,128]{2,1,0:T(8,128)(2,1)S(1)}, bf16[32,16,128]{2,1,0:T(8,128)(2,1)S(1)}, u32[]{:S(2)}, u32[]{:S(2)}) collective-permute-start(bf16[32,16,128]{2,1,0:T(8,128)(2,1)S(1)} %all_to_all.11.own), channel_id=1, source_target_pairs={{0,4},{4,0},{1,5},{5,1},{2,6},{6,2},{3,7},{7,3},{8,12},{12,8},{9,1... | collective-permute-start | bytes 393224 | tf_op jit(solution)/shard_map/ppermute | solution.py:399
  59.0 3.7 %collective-permute-start.5 = (f32[2,8,112]{2,1,0:T(8,128)S(1)}, f32[2,8,112]{2,1,0:T(8,128)S(1)}, u32[]{:S(2)}, u32[]{:S(2)}) collective-permute-start(f32[2,8,112]{2,1,0:T(8,128)S(1)} %get-tuple-element.22), channel_id=1, source_target_pairs={{0,1},{1,2},{2,3},{3,0},{4,5},{5,6},{6,7},{7,4},{8,9},{9,10},{10,1... | collective-permute-start | bytes 21512 | tf_op jit(solution)/shard_map/ppermute | solution.py:411
  59.6 5.2 %collective-permute-start.6 = (f32[2,8,112]{2,1,0:T(8,128)S(1)}, f32[2,8,112]{2,1,0:T(8,128)S(1)}, u32[]{:S(2)}, u32[]{:S(2)}) collective-permute-start(f32[2,8,112]{2,1,0:T(8,128)S(1)} %get-tuple-element.23), channel_id=1, source_target_pairs={{0,2},{1,3},{2,0},{3,1},{4,6},{5,7},{6,4},{7,5},{8,10},{9,11},{10,... | collective-permute-start | bytes 21512 | tf_op jit(solution)/shard_map/ppermute | solution.py:411
  62.0 4.9 %collective-permute-start.7 = (f32[2,8,112]{2,1,0:T(8,128)S(1)}, f32[2,8,112]{2,1,0:T(8,128)S(1)}, u32[]{:S(2)}, u32[]{:S(2)}) collective-permute-start(f32[2,8,112]{2,1,0:T(8,128)S(1)} %get-tuple-element.24), channel_id=1, source_target_pairs={{0,3},{1,0},{2,1},{3,2},{4,7},{5,4},{6,5},{7,6},{8,11},{9,8},{10,9... | collective-permute-start | bytes 21512 | tf_op jit(solution)/shard_map/ppermute | solution.py:411

commit v2 on v1

v2 whole, which is shorter than its diff:
```python
import functools

import jax
import jax.numpy as jnp
from jax import lax
from jax.experimental import pallas as pl
from jax.experimental.pallas import tpu as pltpu
from jax.sharding import Mesh
from jax.sharding import PartitionSpec as P

BLOCK = 128
LATENT = 512
HEADS = 16
ROWS = 32
ITEMS = HEADS * ROWS
ROW_STRIDE = 40
HEAD_STRIDE = 24
LANES = 128
UNROLL = 8
PAIRS = 24
LIST = 64
NONE = -1e30
MASKED = -3e38
F32 = jnp.float32
BF16 = jnp.bfloat16


def dot_t(a, b):
    return lax.dot_general(a, b, (((1,), (1,)), ((), ())), preferred_element_type=F32)


def dot(a, b):
    return jnp.dot(a, b, preferred_element_type=F32)


def split3(x):
    hi = x.astype(BF16).astype(F32)
    mid = (x - hi).astype(BF16).astype(F32)
    return hi, mid, x - hi - mid


def pack_stats(peak, total):
    lane = lax.broadcasted_iota(jnp.int32, peak.shape, 1) // 16
    parts = split3(peak) + split3(total)
    out = parts[0]
    for i in range(1, 6):
        out = jnp.where(lane == i, parts[i], out)
    return out.astype(BF16)


def spread_stats(packed, lanes_each):
    part = lax.broadcasted_iota(jnp.int32, (LANES, 2 * LANES), 0)
    side = lax.broadcasted_iota(jnp.int32, (LANES, 2 * LANES), 1) // LANES
    used = (part % 16 < lanes_each) & (part // 48 == side) & (part < 96)
    both = dot(packed, used.astype(BF16))
    return both[:, :LANES], both[:, LANES:]


def own_lanes(stats):
    lane = lax.broadcasted_iota(jnp.int32, stats.shape, 2) % 16
    return jnp.where(lane == lax.broadcasted_iota(jnp.int32, stats.shape, 1), stats, 0.0)


def widen_rope(rope, rope_wide):
    tok = lax.broadcasted_iota(jnp.int32, (BLOCK, BLOCK // 2), 0)
    pair = lax.broadcasted_iota(jnp.int32, (BLOCK, BLOCK // 2), 1)
    spread = (tok // 2 == pair).astype(BF16)
    half = (
        lax.broadcasted_iota(jnp.int32, (BLOCK, LANES), 1) // (LANES // 2)
        == lax.broadcasted_iota(jnp.int32, (BLOCK, LANES), 0) % 2
    )
    for b in range(16):
        wide = dot(spread, rope[b * 64 : (b + 1) * 64, :])
        rope_wide[b * BLOCK : (b + 1) * BLOCK, :] = jnp.where(half, wide, 0.0).astype(BF16)


def place(code):
    row = code >> 4
    heads = pl.ds(pl.multiple_of(row * HEAD_STRIDE, 8), HEADS)
    where = pl.ds(row, HEADS, stride=ROW_STRIDE)
    tokens = pl.ds(pl.multiple_of((code & 15) * BLOCK, BLOCK), BLOCK)
    return heads, where, tokens


def chunks_of(count):
    return (count + UNROLL - 1) // UNROLL


def score_pairs(pairs, side, q_lat, q_rot, latent, rope_wide, scores, peak, scale):
    count = pairs[side, LIST - 1]

    def step(c, _):
        for u in range(UNROLL):
            p = c * UNROLL + u
            heads, where, tokens = place(pairs[side, p])
            query = jnp.concatenate([q_lat[j, heads, :] for j in range(4)], axis=1).astype(BF16)
            s = dot_t(latent[tokens, :], query) + dot_t(
                rope_wide[tokens, :], q_rot[heads, :].astype(BF16)
            )
            s = jnp.where(p < count, s.T * scale, MASKED)
            scores[p] = s
            peak[where, :] = jnp.maximum(peak[where, :], s)
        return 0

    lax.fori_loop(0, chunks_of(count), step, 0)


def prepare_kernel(
    chosen_hbm, q_nope_hbm, q_rope_hbm, key_hbm, latent_hbm, rope_hbm,
    q_lat, q_rot, scores, peak, latent, pairs,
    chosen, found, q_nope, q_rope, key, rope, rope_wide, sems, *, scale
):
    core = lax.axis_index("core")
    device = (lax.axis_index("y") * 8 + lax.axis_index("z")) * 2 + core
    mine = pl.ds(pl.multiple_of(core * ROWS, ROWS), ROWS)
    copies = [
        pltpu.make_async_copy(src, dst, sems.at[i])
        for i, (src, dst) in enumerate(
            (
                (chosen_hbm.at[core], chosen),
                (q_nope_hbm.at[mine], q_nope),
                (q_rope_hbm.at[mine], q_rope),
                (rope_hbm, rope),
                (key_hbm, key),
                (latent_hbm, latent),
            )
        )
    ]
    for copy in copies:
        copy.start()
    copies[0].wait()

    def find(r, count):
        offset = (r - (device >> 1)) * 32
        for k in range(16):
            block = chosen[k, r]
            found[count] = block + offset
            count = count + ((block >> 5) == (device >> 1)).astype(jnp.int32)
        return count

    def deal(p, counts):
        code = found[p]
        side = ((code >> 4) & 1) ^ core
        pairs[side, jnp.where(side == 0, counts[0], counts[1])] = ((code >> 5) << 4) + (code & 15)
        return counts[0] + (1 - side), counts[1] + side

    count = lax.fori_loop(0, 20, find, jnp.int32(0), unroll=2)
    for copy in copies[1:5]:
        copy.wait()
    for r in range(20, ROWS):
        count = find(r, count)
    low = lax.broadcasted_iota(jnp.int32, (ROWS, LANES), 1) < LANES // 2
    for g in range(HEADS // 2):
        two = q_rope[:, g * LANES : (g + 1) * LANES].astype(F32)
        turned = pltpu.roll(two, LANES // 2, 1)
        q_rot[pl.ds(2 * g, ROWS, stride=HEAD_STRIDE), :] = jnp.where(low, two, turned)
        q_rot[pl.ds(2 * g + 1, ROWS, stride=HEAD_STRIDE), :] = jnp.where(low, turned, two)
    for h in range(HEADS):
        wide = dot(q_nope[:, h * LANES : (h + 1) * LANES], key[h])
        for j in range(4):
            q_lat[j, pl.ds(h, ROWS, stride=HEAD_STRIDE), :] = wide[:, j * LANES : (j + 1) * LANES]
    widen_rope(rope, rope_wide)
    peak[...] = jnp.full_like(peak, NONE)
    counts = lax.fori_loop(0, count, deal, (jnp.int32(0), jnp.int32(0)))
    for side in range(2):
        for i in range(UNROLL):
            pairs[side, counts[side] + i] = 0
        pairs[side, LIST - 1] = counts[side]
    copies[5].wait()
    score_pairs(pairs, 0, q_lat, q_rot, latent, rope_wide, scores, peak, scale)


def gather_lanes(stats, copies):
    n = stats.shape[0] // 16
    kept = own_lanes(stats.astype(F32).reshape(n, 16, LANES)).reshape(n * 16, LANES).astype(BF16)
    row = lax.broadcasted_iota(jnp.int32, (n * copies, n * 16), 0) // copies
    item = lax.broadcasted_iota(jnp.int32, (n * copies, n * 16), 1) // 16
    return dot((row == item).astype(BF16), kept).astype(BF16)


def attend_kernel(
    pairs, q_lat, q_rot, scores, peak_own, latent, latent_sib, rope_sib, value, value_sib,
    out0, out1, out2, out3,
    rope_wide, scores_sib, peak, acc, total, stats, *, scale
):
    core = lax.axis_index("core")
    me = lax.axis_index("y")
    n = 16
    widen_rope(rope_sib, rope_wide)
    acc[...] = jnp.zeros_like(acc)
    total[...] = jnp.zeros_like(total)
    peak[...] = peak_own[...]
    score_pairs(pairs, 1, q_lat, q_rot, latent_sib, rope_wide, scores_sib, peak, scale)
    heads = [pl.ds(h * ROW_STRIDE, ROWS) for h in range(HEADS)]
    for part in heads:
        peak[part, :] = jnp.broadcast_to(jnp.max(peak[part, :], axis=1, keepdims=True), (ROWS, LANES))

    for side, (raw, keys) in enumerate(((scores, latent), (scores_sib, latent_sib))):

        def step(c, _):
            for u in range(UNROLL):
                p = c * UNROLL + u
                _, where, tokens = place(pairs[side, p])
                shifted = jnp.exp(raw[p] - peak[where, :])
                total[where, :] += shifted
                out = dot(shifted.astype(BF16), keys[tokens, :])
                for j in range(4):
                    acc[j, where, :] += out[:, j * LANES : (j + 1) * LANES]
            return 0

        lax.fori_loop(0, chunks_of(pairs[side, LIST - 1]), step, 0)

    tops = jnp.concatenate([peak[part, :] for part in heads], axis=0)
    sums = jnp.concatenate([total[part, :] for part in heads], axis=0)
    sums = jnp.broadcast_to(jnp.sum(sums, axis=1, keepdims=True), (ITEMS, LANES))
    stats[...] = gather_lanes(pack_stats(tops, sums), 2).astype(F32)
    for k, out in enumerate((out0, out1, out2, out3)):
        to = (me + k) & 3
        for g in range(8):
            first = to * (4 * ROW_STRIDE) + (g // 2) * ROW_STRIDE + (g % 2) * n
            here = pl.ds(pl.multiple_of(first, 8), n)
            for j in range(4):
                out[g * 64 + j * n : g * 64 + (j + 1) * n, :] = acc[j, here, :].astype(BF16)
        for i in range(2):
            here = pl.ds(pl.multiple_of(to * 32 + i * n, n), n)
            own, sib = value[here, :].astype(F32), value_sib[here, :].astype(F32)
            first = jnp.where(core == 0, own, sib)
            second = jnp.where(core == 0, sib, own)
            for u in range(2):
                rows = slice(u * 8, u * 8 + 8)
                piece = jnp.concatenate([first[rows], second[rows]], axis=0).astype(BF16)
                at = 512 + (2 * i + u) * n
                out[at : at + n, :] = piece
        out[576:592, :] = stats[pl.ds(pl.multiple_of(to * 16, 16), 16), :].astype(BF16)


def cross_kernel(own, got1, got2, got3, out):
    me = lax.axis_index("y")
    n = 16
    sources = (own, got1, got2, got3)
    packed = []
    for src in sources:
        rows = src[576:592, :].astype(F32).reshape(8, 2, LANES)[:, :1]
        packed.append(own_lanes(jnp.broadcast_to(rows, (8, n, LANES))).reshape(128, LANES))
    tops, sums = spread_stats(jnp.concatenate(packed, axis=0).astype(BF16), n)
    tops, sums = tops.reshape(4, 128, LANES), sums.reshape(4, 128, LANES)
    top = jnp.max(tops, axis=0)
    factors = jnp.exp(tops - top[None])
    stats = pack_stats(top, jnp.sum(factors * sums, axis=0))
    out[:, 128:136, :] = gather_lanes(stats, 8).reshape(8, 8, LANES)
    for g in range(8):
        for j in range(4):
            here = slice(g * 64 + j * n, g * 64 + (j + 1) * n)
            total = jnp.zeros((n, LANES), F32)
            for k, src in enumerate(sources):
                total += src[here, :].astype(F32) * factors[k, g * n : (g + 1) * n]
            out[g, j * n : (j + 1) * n, :] = total.astype(BF16)
        for k, src in enumerate(sources):
            origin = (me + 4 - k) & 3
            at = 512 + (g // 2) * n
            out[g, pl.ds(pl.multiple_of(64 + origin * n, n), n), :] = src[at : at + n, :]


def merge_kernel(got, out):
    packed = got[:, 128:136, :].astype(F32)
    packed = own_lanes(jnp.concatenate([packed, packed], axis=1)).astype(BF16)
    tops, sums = (x.reshape(8, 16, LANES) for x in spread_stats(packed.reshape(128, LANES), 16))
    factors = jnp.exp(tops - jnp.max(tops, axis=0, keepdims=True))
    total = jnp.sum(factors * sums, axis=0)
    result = jnp.zeros((16, LANES), F32)
    for j in range(4):
        merged = jnp.sum(got[:, j * 16 : (j + 1) * 16, :].astype(F32) * factors, axis=0)
        value = got[:, 64 + j * 16 : 80 + j * 16, :].reshape(128, LANES)
        for part in split3(merged):
            result += dot(part.astype(BF16), value)
    result = (result / total).astype(BF16)
    for s in range(32):
        out[s] = result


def project_kernel(own, sib, weight, *outs):
    core = lax.axis_index("core")
    me = lax.axis_index("head")
    zero = core == 0
    total = jnp.zeros((2 * ROWS, weight.shape[0]), F32)
    for h in range(HEADS):
        mine = own[2 * h : 2 * h + 2].reshape(ROWS, LANES)
        other = sib[2 * h : 2 * h + 2].reshape(ROWS, LANES)
        rows = jnp.concatenate([jnp.where(zero, mine, other), jnp.where(zero, other, mine)], axis=0)
        total += dot_t(rows, weight[:, h * LANES : (h + 1) * LANES])
    total = total.reshape(2, 4, 8, weight.shape[0])
    for k in range(4):
        want = lax.rem(me + k, 4)
        part = total[:, 0]
        for i in range(1, 4):
            part = jnp.where(want == i, total[:, i], part)
        outs[k][...] = part


VMEM = pl.BlockSpec(memory_space=pltpu.VMEM)
SMEM = pl.BlockSpec(memory_space=pltpu.SMEM)
HBM = pl.BlockSpec(memory_space=pltpu.HBM)


def params(mebibytes=8):
    return pltpu.CompilerParams(vmem_limit_bytes=mebibytes * 1024 * 1024)


def body(
    query_nope, query_rope, key_up, cache_latent, cache_rope, chosen_blocks, value_up, output_weight
):
    steps, rows, _ = query_nope.shape
    heads, nope, latent = key_up.shape
    rot = cache_rope.shape[1] // 2
    scale = (nope + rot) ** (-0.5)
    swap = [(0, 1), (1, 0)]
    value = value_up.reshape(-1, LANES)
    n_rows = steps * rows
    def from_sibling(x):
        return lax.ppermute(x, "core", swap)

    latent_sib, rope_sib, value_sib = (
        from_sibling(cache_latent),
        from_sibling(cache_rope),
        from_sibling(value),
    )
    slots = PAIRS + UNROLL
    q_lat, q_rot, scores, peak, latent_own, pairs = pl.pallas_call(
        functools.partial(prepare_kernel, scale=scale),
        out_shape=(
            jax.ShapeDtypeStruct((4, rows * HEAD_STRIDE, LANES), F32),
            jax.ShapeDtypeStruct((rows * HEAD_STRIDE, LANES), F32),
            jax.ShapeDtypeStruct((slots, heads, LANES), F32),
            jax.ShapeDtypeStruct((heads * ROW_STRIDE, LANES), F32),
            jax.ShapeDtypeStruct(cache_latent.shape, BF16),
            jax.ShapeDtypeStruct((2, LIST), jnp.int32),
        ),
        in_specs=[HBM] * 6,
        out_specs=(VMEM,) * 5 + (SMEM,),
        scratch_shapes=[
            pltpu.SMEM((chosen_blocks.shape[2], rows), jnp.int32),
            pltpu.SMEM((LIST,), jnp.int32),
            pltpu.VMEM((rows, heads * nope), BF16),
            pltpu.VMEM((rows, heads * rot), BF16),
            pltpu.VMEM(key_up.shape, BF16),
            pltpu.VMEM(cache_rope.shape, BF16),
            pltpu.VMEM((cache_latent.shape[0], LANES), BF16),
            pltpu.SemaphoreType.DMA((6,)),
        ],
        compiler_params=params(20),
        name="prepare",
    )(
        *(
            pltpu.with_memory_space_constraint(x, pltpu.HBM)
            for x in (
                chosen_blocks.transpose(0, 2, 1),
                query_nope.reshape(n_rows, -1),
                query_rope.reshape(n_rows, -1),
                key_up,
                cache_latent,
                cache_rope,
            )
        )
    )
    blocks = pl.pallas_call(
        functools.partial(attend_kernel, scale=scale),
        out_shape=(jax.ShapeDtypeStruct((592, LANES), BF16),) * 4,
        in_specs=[SMEM] + [VMEM] * 9,
        out_specs=(VMEM,) * 4,
        scratch_shapes=[
            pltpu.VMEM((cache_latent.shape[0], LANES), BF16),
            pltpu.VMEM((slots, heads, LANES), F32),
            pltpu.VMEM((heads * ROW_STRIDE, LANES), F32),
            pltpu.VMEM((4, heads * ROW_STRIDE, LANES), F32),
            pltpu.VMEM((heads * ROW_STRIDE, LANES), F32),
            pltpu.VMEM((64, LANES), F32),
        ],
        compiler_params=params(20),
        name="attend",
    )(pairs, q_lat, q_rot, scores, peak, latent_own, latent_sib, rope_sib, value, value_sib)
    got = [
        lax.ppermute(blocks[k], "y", [(i, (i + k) % 4) for i in range(4)]) for k in range(1, 4)
    ]
    packed = pl.pallas_call(
        cross_kernel,
        out_shape=jax.ShapeDtypeStruct((8, 136, LANES), BF16),
        in_specs=[VMEM] * 4,
        out_specs=VMEM,
        compiler_params=params(),
        name="cross",
    )(blocks[0], *got)
    parts = lax.all_to_all(packed, "z", 0, 0)
    values = pl.pallas_call(
        merge_kernel,
        out_shape=jax.ShapeDtypeStruct((32, 16, LANES), BF16),
        in_specs=[VMEM],
        out_specs=VMEM,
        compiler_params=params(),
        name="merge",
    )(parts)
    own = lax.all_to_all(values, ("y", "z"), 0, 0)
    sib = lax.ppermute(own, "core", swap)
    width = output_weight.shape[1]
    terms = pl.pallas_call(
        project_kernel,
        out_shape=(jax.ShapeDtypeStruct((steps, rows // 4, width), F32),) * 4,
        in_specs=[VMEM] * 3,
        out_specs=(VMEM,) * 4,
        compiler_params=params(),
        name="project",
    )(own, sib, output_weight.transpose(1, 0))
    out = terms[0]
    for k in range(1, 4):
        out = out + lax.ppermute(terms[k], "head", [(i, (i + k) % 4) for i in range(4)])
    return out.astype(BF16)


def solution(mesh):
    fine = Mesh(mesh.devices.reshape(4, 8, 2, 4), ("y", "z", "core", "head"))
    ctx = ("y", "z", "core")
    placed = (
        P(None, None, "head"),
        P(None, None, "head"),
        P("head", None, None),
        P(ctx, None),
        P(ctx, None),
        P(),
        P("head", ctx, None),
        P("head", ctx),
    )
    return jax.shard_map(
        body, mesh=fine, in_specs=placed, out_specs=P(None, "head", ctx), check_vma=False
    )
```

time: 67.6 us -> 66.7 us (0.987)
  waiting for transfers between devices: 13.2 us -> 11.7 us
  blocking collectives: 33.9 us -> 35 us
    pallas_call x1, Pallas kernels: 6.03 us -> 2.38 us  [body(): pl.pallas_call(functools.partial(attend_kernel, scale=scale), out_shape=(...]
    pallas_call x1, Pallas kernels: 0.78 us -> 3.95 us  [body(): pl.pallas_call(functools.partial(prepare_kernel, scale=scale), out_shape=...]
    ppermute x1 -> x3, waiting for transfers between devices: 2.13 us -> 0.32 us  [from_sibling(): return lax.ppermute(x, 'core', swap)]
    all_to_all x1, blocking collectives: 19.2 us -> 20.5 us  [body(): parts = lax.all_to_all(packed, 'z', 0, 0)]
  transfers between devices with their start and end apart: 8 -> 10, of which waited for: 6 -> 8; matrix products, arithmetic and copies ran while one was open for 0% -> 0% of each run, Pallas kernels for 0% -> 6%
where the time goes in v2:
time: 66.7 us; the launch traced here: 66.4 us
  blocking collectives  35 us (52%)
  waiting for transfers between devices  11.7 us (18%)
  starting transfers between devices  11.3 us (17%)
  Pallas kernels  7.67 us (11%)
    all_to_all x1, blocking collectives, body(): parts = lax.all_to_all(packed, 'z', 0, 0)  20.5 us
    all_to_all x1, blocking collectives, body(): own = lax.all_to_all(values, ('y', 'z'), 0, 0)  14.5 us
    ppermute x3, starting transfers between devices, body(): lax.ppermute(blocks[k], 'y', [(i, (i + k) % 4) for i in range(4)])  7.89 us
    ppermute x3, waiting for transfers between devices, body(): lax.ppermute(blocks[k], 'y', [(i, (i + k) % 4) for i in range(4)])  5.18 us
    ppermute x3, waiting for transfers between devices, body(): lax.ppermute(terms[k], 'head', [(i, (i + k) % 4) for i in range(4)])  4.86 us
    pallas_call x1, Pallas kernels, body(): pl.pallas_call(functools.partial(prepare_kernel, scale=scale), out_shape=...  3.95 us
    ppermute x3, starting transfers between devices, body(): lax.ppermute(terms[k], 'head', [(i, (i + k) % 4) for i in range(4)])  2.94 us
    pallas_call x1, Pallas kernels, body(): pl.pallas_call(functools.partial(attend_kernel, scale=scale), out_shape=(...  2.38 us
  transfers between devices with their start and end apart: 10, of which 8 were waited for; matrix products, arithmetic and copies ran while one was open for 0% of the time, Pallas kernels for 6%

profile of v2, /device:TPU:6, one launch (start us, length us, event | category | flops | bytes accessed | tf_op | source)
XLA Modules:
  0.0 66.4 jit_solution(1742997269629799318)
XLA Ops:
  0.0 0.0 collective-permute-start
  0.0 0.5 collective-permute-start.1
  0.5 0.0 collective-permute-start.2
  0.5 0.0 copy-start.1
  0.5 3.9 %prepare.1 = (f32[4,768,128]{2,1,0:T(8,128)S(1)}, f32[768,128]{1,0:T(8,128)S(1)}, f32[32,16,128]{2,1,0:T(8,128)S(1)}, f32[640,128]{1,0:T(8,128)S(1)}, bf16[2048,...) custom-call(s32[2,16,32]{2,1,0:T(8,128)} %bitcast.10, bf16[64,2048]{1,0:T(8,128)(2,1)} %bitcast.8, bf16[64,1024]{1,0:T(8,128)(2,1)} %bitcast.9, ...), custom_call_target="tpu_custom_call" | custom-call | tf_op jit(solution)/shard_map/prepare/pallas_call | solution.py:328
  4.5 0.3 collective-permute-done.2.value_sib
  4.8 0.0 collective-permute-done.1.rope_sib
  4.8 0.0 collective-permute-done.latent_sib
  4.8 0.0 copy-done.1
  4.8 2.4 %attend.1 = (bf16[592,128]{1,0:T(8,128)(2,1)S(1)}, bf16[592,128]{1,0:T(8,128)(2,1)S(1)}, bf16[592,128]{1,0:T(8,128)(2,1)S(1)}, bf16[592,128]{1,0:T(8,128)(2,1)S(1)}) custom-call(s32[2,64]{1,0:T(2,128)S(1)} %get-tuple-element.19.pairs, f32[4,768,128]{2,1,0:T(8,128)S(1)} %get-tuple-element.20.q_lat, f32[768,128]{1,0:T(8,128)S(1)} %get-tuple-element.21.q_rot, ...), custom_call_target="tpu_custom_call" | custom-call | tf_op jit(solution)/shard_map/attend/pallas_call | solution.py:365
  7.2 0.0 copy-start
  7.2 1.6 %collective-permute-start.3 = (bf16[592,128]{1,0:T(8,128)(2,1)S(1)}, bf16[592,128]{1,0:T(8,128)(2,1)S(1)}, u32[]{:S(2)}, u32[]{:S(2)}) collective-permute-start(bf16[592,128]{1,0:T(8,128)(2,1)S(1)} %get-tuple-element.26), channel_id=1, source_target_pairs={{0,64},{64,128},{128,192},{192,0},{1,65},{65,129},{129,193},{193,1... | collective-permute-start | bytes 454664 | tf_op jit(solution)/shard_map/ppermute | solution.py:382
  8.8 6.2 %collective-permute-start.4 = (bf16[592,128]{1,0:T(8,128)(2,1)S(1)}, bf16[592,128]{1,0:T(8,128)(2,1)S(1)}, u32[]{:S(2)}, u32[]{:S(2)}) collective-permute-start(bf16[592,128]{1,0:T(8,128)(2,1)S(1)} %get-tuple-element.27), channel_id=1, source_target_pairs={{0,128},{64,192},{128,0},{192,64},{1,129},{65,193},{129,1},{193,65... | collective-permute-start | bytes 454664 | tf_op jit(solution)/shard_map/ppermute | solution.py:382
  15.1 0.0 collective-permute-start.5
  15.1 2.3 %collective-permute-done.3.got1 = bf16[592,128]{1,0:T(8,128)(2,1)S(1)} collective-permute-done((bf16[592,128]{1,0:T(8,128)(2,1)S(1)}, bf16[592,128]{1,0:T(8,128)(2,1)S(1)}, u32[]{:S(2)}, u32[]{:S(2)}) %collective-permute-start.3) | collective-permute-done | bytes 151584 | tf_op jit(solution)/shard_map/ppermute | solution.py:382
  17.4 2.5 %collective-permute-done.4.got2 = bf16[592,128]{1,0:T(8,128)(2,1)S(1)} collective-permute-done((bf16[592,128]{1,0:T(8,128)(2,1)S(1)}, bf16[592,128]{1,0:T(8,128)(2,1)S(1)}, u32[]{:S(2)}, u32[]{:S(2)}) %collective-permute-start.4) | collective-permute-done | bytes 151584 | tf_op jit(solution)/shard_map/ppermute | solution.py:382
  19.9 0.4 collective-permute-done.5.got3
  20.3 0.5 cross.1
  20.8 20.5 %all_to_all.10.got = bf16[8,136,128]{2,1,0:T(8,128)(2,1)S(1)} all-to-all(bf16[8,136,128]{2,1,0:T(8,128)(2,1)S(1)} %cross.1), channel_id=1, replica_groups=mesh['y'=4,'z'=8,'core'=2,'head'=4] {'z'}, dimensions={0} | all-to-all | bytes 557056 | tf_op jit(solution)/shard_map/all_to_all | solution.py:392
  41.3 0.4 merge.1
  41.8 14.5 %all_to_all.11.own = bf16[32,16,128]{2,1,0:T(8,128)(2,1)S(1)} all-to-all(bf16[32,16,128]{2,1,0:T(8,128)(2,1)S(1)} %merge.1), channel_id=1, replica_groups=mesh['y'=4,'z'=8,'core'=2,'head'=4] {'y','z'}, dimensions={0} | all-to-all | bytes 262144 | tf_op jit(solution)/shard_map/all_to_all | solution.py:401
  56.2 0.0 collective-permute-start.6
  56.2 1.3 %collective-permute-done.6.sib = bf16[32,16,128]{2,1,0:T(8,128)(2,1)S(1)} collective-permute-done((bf16[32,16,128]{2,1,0:T(8,128)(2,1)S(1)}, bf16[32,16,128]{2,1,0:T(8,128)(2,1)S(1)}, u32[]{:S(2)}, u32[]{:S(2)}) %collective-permute-start.6) | collective-permute-done | bytes 131104 | tf_op jit(solution)/shard_map/ppermute | solution.py:402
  57.6 0.0 copy-done
  57.6 0.4 project.1
  58.0 0.5 collective-permute-start.7
  58.5 2.4 %collective-permute-start.8 = (f32[2,8,112]{2,1,0:T(8,128)S(1)}, f32[2,8,112]{2,1,0:T(8,128)S(1)}, u32[]{:S(2)}, u32[]{:S(2)}) collective-permute-start(f32[2,8,112]{2,1,0:T(8,128)S(1)} %get-tuple-element.31), channel_id=1, source_target_pairs={{0,2},{1,3},{2,0},{3,1},{4,6},{5,7},{6,4},{7,5},{8,10},{9,11},{10,... | collective-permute-start | bytes 21512 | tf_op jit(solution)/shard_map/ppermute | solution.py:414
  60.9 0.0 collective-permute-start.9
  60.9 0.8 %collective-permute-done.7 = f32[2,8,112]{2,1,0:T(8,128)S(1)} collective-permute-done((f32[2,8,112]{2,1,0:T(8,128)S(1)}, f32[2,8,112]{2,1,0:T(8,128)S(1)}, u32[]{:S(2)}, u32[]{:S(2)}) %collective-permute-start.7) | collective-permute-done | bytes 7200 | tf_op jit(solution)/shard_map/ppermute | solution.py:414
  61.7 2.0 %collective-permute-done.8 = f32[2,8,112]{2,1,0:T(8,128)S(1)} collective-permute-done((f32[2,8,112]{2,1,0:T(8,128)S(1)}, f32[2,8,112]{2,1,0:T(8,128)S(1)}, u32[]{:S(2)}, u32[]{:S(2)}) %collective-permute-start.8) | collective-permute-done | bytes 7200 | tf_op jit(solution)/shard_map/ppermute | solution.py:414
  63.7 2.1 %collective-permute-done.9 = f32[2,8,112]{2,1,0:T(8,128)S(1)} collective-permute-done((f32[2,8,112]{2,1,0:T(8,128)S(1)}, f32[2,8,112]{2,1,0:T(8,128)S(1)}, u32[]{:S(2)}, u32[]{:S(2)}) %collective-permute-start.9) | collective-permute-done | bytes 7200 | tf_op jit(solution)/shard_map/ppermute | solution.py:414
  65.8 0.6 add_convert_fusion
Async XLA Ops:
  0.0 4.8 %collective-permute-start = (bf16[2048,512]{1,0:T(8,128)(2,1)}, bf16[2048,512]{1,0:T(8,128)(2,1)S(1)}, u32[]{:S(2)}, u32[]{:S(2)}) collective-permute-start(bf16[2048,512]{1,0:T(8,128)(2,1)} %latent_hbm.1), channel_id=1, source_target_pairs={{0,4},{4,0},{1,5},{5,1},{2,6},{6,2},{3,7},{7,3},{8,12},{12,8},{9,1... | collective-permute-start | bytes 6291464 | tf_op jit(solution)/shard_map/ppermute | solution.py:320
  0.0 4.8 %collective-permute-start.1 = (bf16[1024,128]{1,0:T(8,128)(2,1)}, bf16[1024,128]{1,0:T(8,128)(2,1)S(1)}, u32[]{:S(2)}, u32[]{:S(2)}) collective-permute-start(bf16[1024,128]{1,0:T(8,128)(2,1)} %rope_hbm.1), channel_id=1, source_target_pairs={{0,4},{4,0},{1,5},{5,1},{2,6},{6,2},{3,7},{7,3},{8,12},{12,8},{9,1... | collective-permute-start | bytes 786440 | tf_op jit(solution)/shard_map/ppermute | solution.py:320
  0.5 4.3 %collective-permute-start.2 = (bf16[128,128]{1,0:T(8,128)(2,1)}, bf16[128,128]{1,0:T(8,128)(2,1)S(1)}, u32[]{:S(2)}, u32[]{:S(2)}) collective-permute-start(bf16[128,128]{1,0:T(8,128)(2,1)} %bitcast.6), channel_id=1, source_target_pairs={{0,4},{4,0},{1,5},{5,1},{2,6},{6,2},{3,7},{7,3},{8,12},{12,8},{9,1... | collective-permute-start | bytes 98312 | tf_op jit(solution)/shard_map/ppermute | solution.py:320
  0.5 4.3 %copy-start.1 = (bf16[16,8,128]{2,1,0:T(8,128)(2,1)S(1)}, bf16[16,8,128]{2,1,0:T(8,128)(2,1)}, u32[]{:S(2)}) copy-start(bf16[16,8,128]{2,1,0:T(8,128)(2,1)} %param.14) | copy-start | bytes 98308
  7.2 50.4 %copy-start = (bf16[2048,112]{0,1:T(8,128)(2,1)S(1)}, bf16[2048,112]{0,1:T(8,128)(2,1)}, u32[]{:S(2)}) copy-start(bf16[2048,112]{0,1:T(8,128)(2,1)} %param.15) | copy-start | bytes 1376260
  7.2 10.2 %collective-permute-start.3 = (bf16[592,128]{1,0:T(8,128)(2,1)S(1)}, bf16[592,128]{1,0:T(8,128)(2,1)S(1)}, u32[]{:S(2)}, u32[]{:S(2)}) collective-permute-start(bf16[592,128]{1,0:T(8,128)(2,1)S(1)} %get-tuple-element.26), channel_id=1, source_target_pairs={{0,64},{64,128},{128,192},{192,0},{1,65},{65,129},{129,193},{193,1... | collective-permute-start | bytes 454664 | tf_op jit(solution)/shard_map/ppermute | solution.py:382
  8.8 11.0 %collective-permute-start.4 = (bf16[592,128]{1,0:T(8,128)(2,1)S(1)}, bf16[592,128]{1,0:T(8,128)(2,1)S(1)}, u32[]{:S(2)}, u32[]{:S(2)}) collective-permute-start(bf16[592,128]{1,0:T(8,128)(2,1)S(1)} %get-tuple-element.27), channel_id=1, source_target_pairs={{0,128},{64,192},{128,0},{192,64},{1,129},{65,193},{129,1},{193,65... | collective-permute-start | bytes 454664 | tf_op jit(solution)/shard_map/ppermute | solution.py:382
  15.1 5.2 %collective-permute-start.5 = (bf16[592,128]{1,0:T(8,128)(2,1)S(1)}, bf16[592,128]{1,0:T(8,128)(2,1)S(1)}, u32[]{:S(2)}, u32[]{:S(2)}) collective-permute-start(bf16[592,128]{1,0:T(8,128)(2,1)S(1)} %get-tuple-element.28), channel_id=1, source_target_pairs={{0,192},{64,0},{128,64},{192,128},{1,193},{65,1},{129,65},{193,129... | collective-permute-start | bytes 454664 | tf_op jit(solution)/shard_map/ppermute | solution.py:382
  56.2 1.3 %collective-permute-start.6 = (bf16[32,16,128]{2,1,0:T(8,128)(2,1)S(1)}, bf16[32,16,128]{2,1,0:T(8,128)(2,1)S(1)}, u32[]{:S(2)}, u32[]{:S(2)}) collective-permute-start(bf16[32,16,128]{2,1,0:T(8,128)(2,1)S(1)} %all_to_all.11.own), channel_id=1, source_target_pairs={{0,4},{4,0},{1,5},{5,1},{2,6},{6,2},{3,7},{7,3},{8,12},{12,8},{9,1... | collective-permute-start | bytes 393224 | tf_op jit(solution)/shard_map/ppermute | solution.py:402
  58.0 3.7 %collective-permute-start.7 = (f32[2,8,112]{2,1,0:T(8,128)S(1)}, f32[2,8,112]{2,1,0:T(8,128)S(1)}, u32[]{:S(2)}, u32[]{:S(2)}) collective-permute-start(f32[2,8,112]{2,1,0:T(8,128)S(1)} %get-tuple-element.30), channel_id=1, source_target_pairs={{0,1},{1,2},{2,3},{3,0},{4,5},{5,6},{6,7},{7,4},{8,9},{9,10},{10,1... | collective-permute-start | bytes 21512 | tf_op jit(solution)/shard_map/ppermute | solution.py:414
  58.5 5.2 %collective-permute-start.8 = (f32[2,8,112]{2,1,0:T(8,128)S(1)}, f32[2,8,112]{2,1,0:T(8,128)S(1)}, u32[]{:S(2)}, u32[]{:S(2)}) collective-permute-start(f32[2,8,112]{2,1,0:T(8,128)S(1)} %get-tuple-element.31), channel_id=1, source_target_pairs={{0,2},{1,3},{2,0},{3,1},{4,6},{5,7},{6,4},{7,5},{8,10},{9,11},{10,... | collective-permute-start | bytes 21512 | tf_op jit(solution)/shard_map/ppermute | solution.py:414
  60.9 4.9 %collective-permute-start.9 = (f32[2,8,112]{2,1,0:T(8,128)S(1)}, f32[2,8,112]{2,1,0:T(8,128)S(1)}, u32[]{:S(2)}, u32[]{:S(2)}) collective-permute-start(f32[2,8,112]{2,1,0:T(8,128)S(1)} %get-tuple-element.32), channel_id=1, source_target_pairs={{0,3},{1,0},{2,1},{3,2},{4,7},{5,4},{6,5},{7,6},{8,11},{9,8},{10,9... | collective-permute-start | bytes 21512 | tf_op jit(solution)/shard_map/ppermute | solution.py:414

commit v3 on v2

--- a/solution.py
+++ b/solution.py
@@ -16,7 +16,7 @@
 ROW_STRIDE = 40
 HEAD_STRIDE = 24
 LANES = 128
-UNROLL = 8
+UNROLL = 12
 PAIRS = 24
 LIST = 64
 NONE = -1e30
@@ -378,9 +378,9 @@
         compiler_params=params(20),
         name="attend",
     )(pairs, q_lat, q_rot, scores, peak, latent_own, latent_sib, rope_sib, value, value_sib)
-    got = [
-        lax.ppermute(blocks[k], "y", [(i, (i + k) % 4) for i in range(4)]) for k in range(1, 4)
-    ]
+    got = {
+        k: lax.ppermute(blocks[k], "y", [(i, (i + k) % 4) for i in range(4)]) for k in (2, 1, 3)
+    }
     packed = pl.pallas_call(
         cross_kernel,
         out_shape=jax.ShapeDtypeStruct((8, 136, LANES), BF16),
@@ -388,7 +388,7 @@
         out_specs=VMEM,
         compiler_params=params(),
         name="cross",
-    )(blocks[0], *got)
+    )(blocks[0], got[1], got[2], got[3])
     parts = lax.all_to_all(packed, "z", 0, 0)
     values = pl.pallas_call(
         merge_kernel,

time: 66.7 us -> 67.1 us (level)
  starting transfers between devices: 11.3 us -> 9.41 us
  waiting for transfers between devices: 11.7 us -> 12.5 us
  blocking collectives: 35 us -> 35.7 us
    ppermute x3, starting transfers between devices: 7.89 us -> 5.92 us  [body(): lax.ppermute(blocks[k], 'y', [(i, (i + k) % 4) for i in range(4)])]
    ppermute x3, waiting for transfers between devices: 5.18 us -> 6.11 us  [body(): lax.ppermute(blocks[k], 'y', [(i, (i + k) % 4) for i in range(4)])]
  transfers between devices with their start and end apart: 10 -> 10, of which waited for: 8 -> 7; matrix products, arithmetic and copies ran while one was open for 0% -> 0% of each run, Pallas kernels for 6% -> 6%
where the time goes in v3:
time: 67.1 us; the launch traced here: 66.4 us
  blocking collectives  35.7 us (53%)
  waiting for transfers between devices  12.5 us (19%)
  starting transfers between devices  9.41 us (14%)
  Pallas kernels  8.22 us (12%)
    all_to_all x1, blocking collectives, body(): parts = lax.all_to_all(packed, 'z', 0, 0)  20.8 us
    all_to_all x1, blocking collectives, body(): own = lax.all_to_all(values, ('y', 'z'), 0, 0)  14.9 us
    ppermute x3, waiting for transfers between devices, body(): lax.ppermute(blocks[k], 'y', [(i, (i + k) % 4) for i in range(4)])  6.11 us
    ppermute x3, starting transfers between devices, body(): lax.ppermute(blocks[k], 'y', [(i, (i + k) % 4) for i in range(4)])  5.92 us
    ppermute x3, waiting for transfers between devices, body(): lax.ppermute(terms[k], 'head', [(i, (i + k) % 4) for i in range(4)])  4.86 us
    pallas_call x1, Pallas kernels, body(): pl.pallas_call(functools.partial(prepare_kernel, scale=scale), out_shape=...  4.14 us
    ppermute x3, starting transfers between devices, body(): lax.ppermute(terms[k], 'head', [(i, (i + k) % 4) for i in range(4)])  2.97 us
    pallas_call x1, Pallas kernels, body(): pl.pallas_call(functools.partial(attend_kernel, scale=scale), out_shape=(...  2.75 us
  transfers between devices with their start and end apart: 10, of which 7 were waited for; matrix products, arithmetic and copies ran while one was open for 0% of the time, Pallas kernels for 6%

profile of v3, /device:TPU:6, one launch (start us, length us, event | category | flops | bytes accessed | tf_op | source)
XLA Modules:
  0.0 66.4 jit_solution(2154539915548988910)
XLA Ops:
  0.0 0.0 collective-permute-start
  0.0 0.5 collective-permute-start.1
  0.5 0.0 collective-permute-start.2
  0.5 0.0 copy-start.1
  0.5 4.1 %prepare.1 = (f32[4,768,128]{2,1,0:T(8,128)S(1)}, f32[768,128]{1,0:T(8,128)S(1)}, f32[36,16,128]{2,1,0:T(8,128)S(1)}, f32[640,128]{1,0:T(8,128)S(1)}, bf16[2048,...) custom-call(s32[2,16,32]{2,1,0:T(8,128)} %bitcast.10, bf16[64,2048]{1,0:T(8,128)(2,1)} %bitcast.8, bf16[64,1024]{1,0:T(8,128)(2,1)} %bitcast.9, ...), custom_call_target="tpu_custom_call" | custom-call | tf_op jit(solution)/shard_map/prepare/pallas_call | solution.py:328
  4.7 0.1 collective-permute-done.2.value_sib
  4.8 0.0 collective-permute-done.1.rope_sib
  4.8 0.0 collective-permute-done.latent_sib
  4.8 0.0 copy-done.1
  4.8 2.7 %attend.1 = (bf16[592,128]{1,0:T(8,128)(2,1)S(1)}, bf16[592,128]{1,0:T(8,128)(2,1)S(1)}, bf16[592,128]{1,0:T(8,128)(2,1)S(1)}, bf16[592,128]{1,0:T(8,128)(2,1)S(1)}) custom-call(s32[2,64]{1,0:T(2,128)S(1)} %get-tuple-element.19.pairs, f32[4,768,128]{2,1,0:T(8,128)S(1)} %get-tuple-element.20.q_lat, f32[768,128]{1,0:T(8,128)S(1)} %get-tuple-element.21.q_rot, ...), custom_call_target="tpu_custom_call" | custom-call | tf_op jit(solution)/shard_map/attend/pallas_call | solution.py:365
  7.6 0.0 copy-start
  7.6 1.6 %collective-permute-start.3 = (bf16[592,128]{1,0:T(8,128)(2,1)S(1)}, bf16[592,128]{1,0:T(8,128)(2,1)S(1)}, u32[]{:S(2)}, u32[]{:S(2)}) collective-permute-start(bf16[592,128]{1,0:T(8,128)(2,1)S(1)} %get-tuple-element.26), channel_id=1, source_target_pairs={{0,64},{64,128},{128,192},{192,0},{1,65},{65,129},{129,193},{193,1... | collective-permute-start | bytes 454664 | tf_op jit(solution)/shard_map/ppermute | solution.py:382
  9.2 2.9 %collective-permute-start.4 = (bf16[592,128]{1,0:T(8,128)(2,1)S(1)}, bf16[592,128]{1,0:T(8,128)(2,1)S(1)}, u32[]{:S(2)}, u32[]{:S(2)}) collective-permute-start(bf16[592,128]{1,0:T(8,128)(2,1)S(1)} %get-tuple-element.27), channel_id=1, source_target_pairs={{0,128},{64,192},{128,0},{192,64},{1,129},{65,193},{129,1},{193,65... | collective-permute-start | bytes 454664 | tf_op jit(solution)/shard_map/ppermute | solution.py:382
  12.1 1.4 %collective-permute-start.5 = (bf16[592,128]{1,0:T(8,128)(2,1)S(1)}, bf16[592,128]{1,0:T(8,128)(2,1)S(1)}, u32[]{:S(2)}, u32[]{:S(2)}) collective-permute-start(bf16[592,128]{1,0:T(8,128)(2,1)S(1)} %get-tuple-element.28), channel_id=1, source_target_pairs={{0,192},{64,0},{128,64},{192,128},{1,193},{65,1},{129,65},{193,129... | collective-permute-start | bytes 454664 | tf_op jit(solution)/shard_map/ppermute | solution.py:382
  13.5 1.7 %collective-permute-done.3.got1 = bf16[592,128]{1,0:T(8,128)(2,1)S(1)} collective-permute-done((bf16[592,128]{1,0:T(8,128)(2,1)S(1)}, bf16[592,128]{1,0:T(8,128)(2,1)S(1)}, u32[]{:S(2)}, u32[]{:S(2)}) %collective-permute-start.3) | collective-permute-done | bytes 151584 | tf_op jit(solution)/shard_map/ppermute | solution.py:382
  15.1 4.4 %collective-permute-done.4.got2 = bf16[592,128]{1,0:T(8,128)(2,1)S(1)} collective-permute-done((bf16[592,128]{1,0:T(8,128)(2,1)S(1)}, bf16[592,128]{1,0:T(8,128)(2,1)S(1)}, u32[]{:S(2)}, u32[]{:S(2)}) %collective-permute-start.4) | collective-permute-done | bytes 151584 | tf_op jit(solution)/shard_map/ppermute | solution.py:382
  19.6 0.0 collective-permute-done.5.got3
  19.6 0.5 cross.1
  20.1 20.8 %all_to_all.10.got = bf16[8,136,128]{2,1,0:T(8,128)(2,1)S(1)} all-to-all(bf16[8,136,128]{2,1,0:T(8,128)(2,1)S(1)} %cross.1), channel_id=1, replica_groups=mesh['y'=4,'z'=8,'core'=2,'head'=4] {'z'}, dimensions={0} | all-to-all | bytes 557056 | tf_op jit(solution)/shard_map/all_to_all | solution.py:392
  40.9 0.4 merge.1
  41.3 14.9 %all_to_all.11.own = bf16[32,16,128]{2,1,0:T(8,128)(2,1)S(1)} all-to-all(bf16[32,16,128]{2,1,0:T(8,128)(2,1)S(1)} %merge.1), channel_id=1, replica_groups=mesh['y'=4,'z'=8,'core'=2,'head'=4] {'y','z'}, dimensions={0} | all-to-all | bytes 262144 | tf_op jit(solution)/shard_map/all_to_all | solution.py:401
  56.2 0.0 collective-permute-start.6
  56.2 1.3 %collective-permute-done.6.sib = bf16[32,16,128]{2,1,0:T(8,128)(2,1)S(1)} collective-permute-done((bf16[32,16,128]{2,1,0:T(8,128)(2,1)S(1)}, bf16[32,16,128]{2,1,0:T(8,128)(2,1)S(1)}, u32[]{:S(2)}, u32[]{:S(2)}) %collective-permute-start.6) | collective-permute-done | bytes 131104 | tf_op jit(solution)/shard_map/ppermute | solution.py:402
  57.6 0.0 copy-done
  57.6 0.4 project.1
  58.0 0.5 collective-permute-start.7
  58.5 2.4 %collective-permute-start.8 = (f32[2,8,112]{2,1,0:T(8,128)S(1)}, f32[2,8,112]{2,1,0:T(8,128)S(1)}, u32[]{:S(2)}, u32[]{:S(2)}) collective-permute-start(f32[2,8,112]{2,1,0:T(8,128)S(1)} %get-tuple-element.31), channel_id=1, source_target_pairs={{0,2},{1,3},{2,0},{3,1},{4,6},{5,7},{6,4},{7,5},{8,10},{9,11},{10,... | collective-permute-start | bytes 21512 | tf_op jit(solution)/shard_map/ppermute | solution.py:414
  61.0 0.0 collective-permute-start.9
  61.0 0.7 %collective-permute-done.7 = f32[2,8,112]{2,1,0:T(8,128)S(1)} collective-permute-done((f32[2,8,112]{2,1,0:T(8,128)S(1)}, f32[2,8,112]{2,1,0:T(8,128)S(1)}, u32[]{:S(2)}, u32[]{:S(2)}) %collective-permute-start.7) | collective-permute-done | bytes 7200 | tf_op jit(solution)/shard_map/ppermute | solution.py:414
  61.7 2.0 %collective-permute-done.8 = f32[2,8,112]{2,1,0:T(8,128)S(1)} collective-permute-done((f32[2,8,112]{2,1,0:T(8,128)S(1)}, f32[2,8,112]{2,1,0:T(8,128)S(1)}, u32[]{:S(2)}, u32[]{:S(2)}) %collective-permute-start.8) | collective-permute-done | bytes 7200 | tf_op jit(solution)/shard_map/ppermute | solution.py:414
  63.7 2.1 %collective-permute-done.9 = f32[2,8,112]{2,1,0:T(8,128)S(1)} collective-permute-done((f32[2,8,112]{2,1,0:T(8,128)S(1)}, f32[2,8,112]{2,1,0:T(8,128)S(1)}, u32[]{:S(2)}, u32[]{:S(2)}) %collective-permute-start.9) | collective-permute-done | bytes 7200 | tf_op jit(solution)/shard_map/ppermute | solution.py:414
  65.8 0.6 add_convert_fusion
Async XLA Ops:
  0.0 4.8 %collective-permute-start = (bf16[2048,512]{1,0:T(8,128)(2,1)}, bf16[2048,512]{1,0:T(8,128)(2,1)S(1)}, u32[]{:S(2)}, u32[]{:S(2)}) collective-permute-start(bf16[2048,512]{1,0:T(8,128)(2,1)} %latent_hbm.1), channel_id=1, source_target_pairs={{0,4},{4,0},{1,5},{5,1},{2,6},{6,2},{3,7},{7,3},{8,12},{12,8},{9,1... | collective-permute-start | bytes 6291464 | tf_op jit(solution)/shard_map/ppermute | solution.py:320
  0.0 4.8 %collective-permute-start.1 = (bf16[1024,128]{1,0:T(8,128)(2,1)}, bf16[1024,128]{1,0:T(8,128)(2,1)S(1)}, u32[]{:S(2)}, u32[]{:S(2)}) collective-permute-start(bf16[1024,128]{1,0:T(8,128)(2,1)} %rope_hbm.1), channel_id=1, source_target_pairs={{0,4},{4,0},{1,5},{5,1},{2,6},{6,2},{3,7},{7,3},{8,12},{12,8},{9,1... | collective-permute-start | bytes 786440 | tf_op jit(solution)/shard_map/ppermute | solution.py:320
  0.5 4.3 %collective-permute-start.2 = (bf16[128,128]{1,0:T(8,128)(2,1)}, bf16[128,128]{1,0:T(8,128)(2,1)S(1)}, u32[]{:S(2)}, u32[]{:S(2)}) collective-permute-start(bf16[128,128]{1,0:T(8,128)(2,1)} %bitcast.6), channel_id=1, source_target_pairs={{0,4},{4,0},{1,5},{5,1},{2,6},{6,2},{3,7},{7,3},{8,12},{12,8},{9,1... | collective-permute-start | bytes 98312 | tf_op jit(solution)/shard_map/ppermute | solution.py:320
  0.5 4.3 %copy-start.1 = (bf16[16,8,128]{2,1,0:T(8,128)(2,1)S(1)}, bf16[16,8,128]{2,1,0:T(8,128)(2,1)}, u32[]{:S(2)}) copy-start(bf16[16,8,128]{2,1,0:T(8,128)(2,1)} %param.14) | copy-start | bytes 98308
  7.6 50.0 %copy-start = (bf16[2048,112]{0,1:T(8,128)(2,1)S(1)}, bf16[2048,112]{0,1:T(8,128)(2,1)}, u32[]{:S(2)}) copy-start(bf16[2048,112]{0,1:T(8,128)(2,1)} %param.15) | copy-start | bytes 1376260
  7.6 7.6 %collective-permute-start.3 = (bf16[592,128]{1,0:T(8,128)(2,1)S(1)}, bf16[592,128]{1,0:T(8,128)(2,1)S(1)}, u32[]{:S(2)}, u32[]{:S(2)}) collective-permute-start(bf16[592,128]{1,0:T(8,128)(2,1)S(1)} %get-tuple-element.26), channel_id=1, source_target_pairs={{0,64},{64,128},{128,192},{192,0},{1,65},{65,129},{129,193},{193,1... | collective-permute-start | bytes 454664 | tf_op jit(solution)/shard_map/ppermute | solution.py:382
  9.2 10.4 %collective-permute-start.4 = (bf16[592,128]{1,0:T(8,128)(2,1)S(1)}, bf16[592,128]{1,0:T(8,128)(2,1)S(1)}, u32[]{:S(2)}, u32[]{:S(2)}) collective-permute-start(bf16[592,128]{1,0:T(8,128)(2,1)S(1)} %get-tuple-element.27), channel_id=1, source_target_pairs={{0,128},{64,192},{128,0},{192,64},{1,129},{65,193},{129,1},{193,65... | collective-permute-start | bytes 454664 | tf_op jit(solution)/shard_map/ppermute | solution.py:382
  12.1 7.5 %collective-permute-start.5 = (bf16[592,128]{1,0:T(8,128)(2,1)S(1)}, bf16[592,128]{1,0:T(8,128)(2,1)S(1)}, u32[]{:S(2)}, u32[]{:S(2)}) collective-permute-start(bf16[592,128]{1,0:T(8,128)(2,1)S(1)} %get-tuple-element.28), channel_id=1, source_target_pairs={{0,192},{64,0},{128,64},{192,128},{1,193},{65,1},{129,65},{193,129... | collective-permute-start | bytes 454664 | tf_op jit(solution)/shard_map/ppermute | solution.py:382
  56.2 1.3 %collective-permute-start.6 = (bf16[32,16,128]{2,1,0:T(8,128)(2,1)S(1)}, bf16[32,16,128]{2,1,0:T(8,128)(2,1)S(1)}, u32[]{:S(2)}, u32[]{:S(2)}) collective-permute-start(bf16[32,16,128]{2,1,0:T(8,128)(2,1)S(1)} %all_to_all.11.own), channel_id=1, source_target_pairs={{0,4},{4,0},{1,5},{5,1},{2,6},{6,2},{3,7},{7,3},{8,12},{12,8},{9,1... | collective-permute-start | bytes 393224 | tf_op jit(solution)/shard_map/ppermute | solution.py:402
  58.0 3.7 %collective-permute-start.7 = (f32[2,8,112]{2,1,0:T(8,128)S(1)}, f32[2,8,112]{2,1,0:T(8,128)S(1)}, u32[]{:S(2)}, u32[]{:S(2)}) collective-permute-start(f32[2,8,112]{2,1,0:T(8,128)S(1)} %get-tuple-element.30), channel_id=1, source_target_pairs={{0,1},{1,2},{2,3},{3,0},{4,5},{5,6},{6,7},{7,4},{8,9},{9,10},{10,1... | collective-permute-start | bytes 21512 | tf_op jit(solution)/shard_map/ppermute | solution.py:414
  58.5 5.2 %collective-permute-start.8 = (f32[2,8,112]{2,1,0:T(8,128)S(1)}, f32[2,8,112]{2,1,0:T(8,128)S(1)}, u32[]{:S(2)}, u32[]{:S(2)}) collective-permute-start(f32[2,8,112]{2,1,0:T(8,128)S(1)} %get-tuple-element.31), channel_id=1, source_target_pairs={{0,2},{1,3},{2,0},{3,1},{4,6},{5,7},{6,4},{7,5},{8,10},{9,11},{10,... | collective-permute-start | bytes 21512 | tf_op jit(solution)/shard_map/ppermute | solution.py:414
  61.0 4.9 %collective-permute-start.9 = (f32[2,8,112]{2,1,0:T(8,128)S(1)}, f32[2,8,112]{2,1,0:T(8,128)S(1)}, u32[]{:S(2)}, u32[]{:S(2)}) collective-permute-start(f32[2,8,112]{2,1,0:T(8,128)S(1)} %get-tuple-element.32), channel_id=1, source_target_pairs={{0,3},{1,0},{2,1},{3,2},{4,7},{5,4},{6,5},{7,6},{8,11},{9,8},{10,9... | collective-permute-start | bytes 21512 | tf_op jit(solution)/shard_map/ppermute | solution.py:414

commit v4 on v3

--- a/solution.py
+++ b/solution.py
@@ -102,7 +102,8 @@
             peak[where, :] = jnp.maximum(peak[where, :], s)
         return 0
 
-    lax.fori_loop(0, chunks_of(count), step, 0)
+    step(0, 0)
+    lax.fori_loop(1, chunks_of(count), step, 0)
 
 
 def prepare_kernel(
@@ -195,20 +196,26 @@
     for part in heads:
         peak[part, :] = jnp.broadcast_to(jnp.max(peak[part, :], axis=1, keepdims=True), (ROWS, LANES))
 
-    for side, (raw, keys) in enumerate(((scores, latent), (scores_sib, latent_sib))):
-
-        def step(c, _):
-            for u in range(UNROLL):
-                p = c * UNROLL + u
-                _, where, tokens = place(pairs[side, p])
-                shifted = jnp.exp(raw[p] - peak[where, :])
-                total[where, :] += shifted
-                out = dot(shifted.astype(BF16), keys[tokens, :])
-                for j in range(4):
-                    acc[j, where, :] += out[:, j * LANES : (j + 1) * LANES]
+    def weigh(side, raw, keys, c):
+        for u in range(UNROLL):
+            p = c * UNROLL + u
+            _, where, tokens = place(pairs[side, p])
+            shifted = jnp.exp(raw[p] - peak[where, :])
+            total[where, :] += shifted
+            out = dot(shifted.astype(BF16), keys[tokens, :])
+            for j in range(4):
+                acc[j, where, :] += out[:, j * LANES : (j + 1) * LANES]
+
+    sides = ((0, scores, latent), (1, scores_sib, latent_sib))
+    for side, raw, keys in sides:
+        weigh(side, raw, keys, 0)
+    for side, raw, keys in sides:
+
+        def step(c, _, side=side, raw=raw, keys=keys):
+            weigh(side, raw, keys, c)
             return 0
 
-        lax.fori_loop(0, chunks_of(pairs[side, LIST - 1]), step, 0)
+        lax.fori_loop(1, chunks_of(pairs[side, LIST - 1]), step, 0)
 
     tops = jnp.concatenate([peak[part, :] for part in heads], axis=0)
     sums = jnp.concatenate([total[part, :] for part in heads], axis=0)

time: 67.1 us -> 66.5 us (level)
  no operation moved by 1% of the time
where the time goes in v4:
time: 66.5 us; the launch traced here: 66.3 us
  blocking collectives  35.7 us (54%)
  waiting for transfers between devices  12.5 us (19%)
  starting transfers between devices  9.36 us (14%)
  Pallas kernels  8.09 us (12%)
    all_to_all x1, blocking collectives, body(): parts = lax.all_to_all(packed, 'z', 0, 0)  21 us
    all_to_all x1, blocking collectives, body(): own = lax.all_to_all(values, ('y', 'z'), 0, 0)  14.7 us
    ppermute x3, waiting for transfers between devices, body(): lax.ppermute(blocks[k], 'y', [(i, (i + k) % 4) for i in range(4)])  6.16 us
    ppermute x3, starting transfers between devices, body(): lax.ppermute(blocks[k], 'y', [(i, (i + k) % 4) for i in range(4)])  5.88 us
    ppermute x3, waiting for transfers between devices, body(): lax.ppermute(terms[k], 'head', [(i, (i + k) % 4) for i in range(4)])  4.86 us
    pallas_call x1, Pallas kernels, body(): pl.pallas_call(functools.partial(prepare_kernel, scale=scale), out_shape=...  4.13 us
    ppermute x3, starting transfers between devices, body(): lax.ppermute(terms[k], 'head', [(i, (i + k) % 4) for i in range(4)])  2.96 us
    pallas_call x1, Pallas kernels, body(): pl.pallas_call(functools.partial(attend_kernel, scale=scale), out_shape=(...  2.62 us
  transfers between devices with their start and end apart: 10, of which 7 were waited for; matrix products, arithmetic and copies ran while one was open for 0% of the time, Pallas kernels for 6%

profile of v4, /device:TPU:6, one launch (start us, length us, event | category | flops | bytes accessed | tf_op | source)
XLA Modules:
  0.0 66.3 jit_solution(6688464620637840445)
XLA Ops:
  0.0 0.0 collective-permute-start
  0.0 0.5 collective-permute-start.1
  0.5 0.0 collective-permute-start.2
  0.5 0.0 copy-start.1
  0.5 4.1 %prepare.1 = (f32[4,768,128]{2,1,0:T(8,128)S(1)}, f32[768,128]{1,0:T(8,128)S(1)}, f32[36,16,128]{2,1,0:T(8,128)S(1)}, f32[640,128]{1,0:T(8,128)S(1)}, bf16[2048,...) custom-call(s32[2,16,32]{2,1,0:T(8,128)} %bitcast.10, bf16[64,2048]{1,0:T(8,128)(2,1)} %bitcast.8, bf16[64,1024]{1,0:T(8,128)(2,1)} %bitcast.9, ...), custom_call_target="tpu_custom_call" | custom-call | tf_op jit(solution)/shard_map/prepare/pallas_call | solution.py:335
  4.7 0.1 collective-permute-done.2.value_sib
  4.8 0.0 collective-permute-done.1.rope_sib
  4.8 0.0 collective-permute-done.latent_sib
  4.8 0.0 copy-done.1
  4.8 2.6 %attend.1 = (bf16[592,128]{1,0:T(8,128)(2,1)S(1)}, bf16[592,128]{1,0:T(8,128)(2,1)S(1)}, bf16[592,128]{1,0:T(8,128)(2,1)S(1)}, bf16[592,128]{1,0:T(8,128)(2,1)S(1)}) custom-call(s32[2,64]{1,0:T(2,128)S(1)} %get-tuple-element.19.pairs, f32[4,768,128]{2,1,0:T(8,128)S(1)} %get-tuple-element.20.q_lat, f32[768,128]{1,0:T(8,128)S(1)} %get-tuple-element.21.q_rot, ...), custom_call_target="tpu_custom_call" | custom-call | tf_op jit(solution)/shard_map/attend/pallas_call | solution.py:372
  7.4 0.0 copy-start
  7.4 1.7 %collective-permute-start.3 = (bf16[592,128]{1,0:T(8,128)(2,1)S(1)}, bf16[592,128]{1,0:T(8,128)(2,1)S(1)}, u32[]{:S(2)}, u32[]{:S(2)}) collective-permute-start(bf16[592,128]{1,0:T(8,128)(2,1)S(1)} %get-tuple-element.26), channel_id=1, source_target_pairs={{0,64},{64,128},{128,192},{192,0},{1,65},{65,129},{129,193},{193,1... | collective-permute-start | bytes 454664 | tf_op jit(solution)/shard_map/ppermute | solution.py:389
  9.1 2.9 %collective-permute-start.4 = (bf16[592,128]{1,0:T(8,128)(2,1)S(1)}, bf16[592,128]{1,0:T(8,128)(2,1)S(1)}, u32[]{:S(2)}, u32[]{:S(2)}) collective-permute-start(bf16[592,128]{1,0:T(8,128)(2,1)S(1)} %get-tuple-element.27), channel_id=1, source_target_pairs={{0,128},{64,192},{128,0},{192,64},{1,129},{65,193},{129,1},{193,65... | collective-permute-start | bytes 454664 | tf_op jit(solution)/shard_map/ppermute | solution.py:389
  12.0 1.3 %collective-permute-start.5 = (bf16[592,128]{1,0:T(8,128)(2,1)S(1)}, bf16[592,128]{1,0:T(8,128)(2,1)S(1)}, u32[]{:S(2)}, u32[]{:S(2)}) collective-permute-start(bf16[592,128]{1,0:T(8,128)(2,1)S(1)} %get-tuple-element.28), channel_id=1, source_target_pairs={{0,192},{64,0},{128,64},{192,128},{1,193},{65,1},{129,65},{193,129... | collective-permute-start | bytes 454664 | tf_op jit(solution)/shard_map/ppermute | solution.py:389
  13.3 1.6 %collective-permute-done.3.got1 = bf16[592,128]{1,0:T(8,128)(2,1)S(1)} collective-permute-done((bf16[592,128]{1,0:T(8,128)(2,1)S(1)}, bf16[592,128]{1,0:T(8,128)(2,1)S(1)}, u32[]{:S(2)}, u32[]{:S(2)}) %collective-permute-start.3) | collective-permute-done | bytes 151584 | tf_op jit(solution)/shard_map/ppermute | solution.py:389
  14.9 4.6 %collective-permute-done.4.got2 = bf16[592,128]{1,0:T(8,128)(2,1)S(1)} collective-permute-done((bf16[592,128]{1,0:T(8,128)(2,1)S(1)}, bf16[592,128]{1,0:T(8,128)(2,1)S(1)}, u32[]{:S(2)}, u32[]{:S(2)}) %collective-permute-start.4) | collective-permute-done | bytes 151584 | tf_op jit(solution)/shard_map/ppermute | solution.py:389
  19.5 0.0 collective-permute-done.5.got3
  19.5 0.5 cross.1
  20.0 21.0 %all_to_all.10.got = bf16[8,136,128]{2,1,0:T(8,128)(2,1)S(1)} all-to-all(bf16[8,136,128]{2,1,0:T(8,128)(2,1)S(1)} %cross.1), channel_id=1, replica_groups=mesh['y'=4,'z'=8,'core'=2,'head'=4] {'z'}, dimensions={0} | all-to-all | bytes 557056 | tf_op jit(solution)/shard_map/all_to_all | solution.py:399
  41.0 0.4 merge.1
  41.4 14.7 %all_to_all.11.own = bf16[32,16,128]{2,1,0:T(8,128)(2,1)S(1)} all-to-all(bf16[32,16,128]{2,1,0:T(8,128)(2,1)S(1)} %merge.1), channel_id=1, replica_groups=mesh['y'=4,'z'=8,'core'=2,'head'=4] {'y','z'}, dimensions={0} | all-to-all | bytes 262144 | tf_op jit(solution)/shard_map/all_to_all | solution.py:408
  56.1 0.0 collective-permute-start.6
  56.1 1.3 %collective-permute-done.6.sib = bf16[32,16,128]{2,1,0:T(8,128)(2,1)S(1)} collective-permute-done((bf16[32,16,128]{2,1,0:T(8,128)(2,1)S(1)}, bf16[32,16,128]{2,1,0:T(8,128)(2,1)S(1)}, u32[]{:S(2)}, u32[]{:S(2)}) %collective-permute-start.6) | collective-permute-done | bytes 131104 | tf_op jit(solution)/shard_map/ppermute | solution.py:409
  57.5 0.0 copy-done
  57.5 0.4 project.1
  57.9 0.5 collective-permute-start.7
  58.4 2.4 %collective-permute-start.8 = (f32[2,8,112]{2,1,0:T(8,128)S(1)}, f32[2,8,112]{2,1,0:T(8,128)S(1)}, u32[]{:S(2)}, u32[]{:S(2)}) collective-permute-start(f32[2,8,112]{2,1,0:T(8,128)S(1)} %get-tuple-element.31), channel_id=1, source_target_pairs={{0,2},{1,3},{2,0},{3,1},{4,6},{5,7},{6,4},{7,5},{8,10},{9,11},{10,... | collective-permute-start | bytes 21512 | tf_op jit(solution)/shard_map/ppermute | solution.py:421
  60.8 0.0 collective-permute-start.9
  60.8 0.8 %collective-permute-done.7 = f32[2,8,112]{2,1,0:T(8,128)S(1)} collective-permute-done((f32[2,8,112]{2,1,0:T(8,128)S(1)}, f32[2,8,112]{2,1,0:T(8,128)S(1)}, u32[]{:S(2)}, u32[]{:S(2)}) %collective-permute-start.7) | collective-permute-done | bytes 7200 | tf_op jit(solution)/shard_map/ppermute | solution.py:421
  61.6 2.0 %collective-permute-done.8 = f32[2,8,112]{2,1,0:T(8,128)S(1)} collective-permute-done((f32[2,8,112]{2,1,0:T(8,128)S(1)}, f32[2,8,112]{2,1,0:T(8,128)S(1)}, u32[]{:S(2)}, u32[]{:S(2)}) %collective-permute-start.8) | collective-permute-done | bytes 7200 | tf_op jit(solution)/shard_map/ppermute | solution.py:421
  63.6 2.1 %collective-permute-done.9 = f32[2,8,112]{2,1,0:T(8,128)S(1)} collective-permute-done((f32[2,8,112]{2,1,0:T(8,128)S(1)}, f32[2,8,112]{2,1,0:T(8,128)S(1)}, u32[]{:S(2)}, u32[]{:S(2)}) %collective-permute-start.9) | collective-permute-done | bytes 7200 | tf_op jit(solution)/shard_map/ppermute | solution.py:421
  65.7 0.6 add_convert_fusion
Async XLA Ops:
  0.0 4.8 %collective-permute-start = (bf16[2048,512]{1,0:T(8,128)(2,1)}, bf16[2048,512]{1,0:T(8,128)(2,1)S(1)}, u32[]{:S(2)}, u32[]{:S(2)}) collective-permute-start(bf16[2048,512]{1,0:T(8,128)(2,1)} %latent_hbm.1), channel_id=1, source_target_pairs={{0,4},{4,0},{1,5},{5,1},{2,6},{6,2},{3,7},{7,3},{8,12},{12,8},{9,1... | collective-permute-start | bytes 6291464 | tf_op jit(solution)/shard_map/ppermute | solution.py:327
  0.0 4.8 %collective-permute-start.1 = (bf16[1024,128]{1,0:T(8,128)(2,1)}, bf16[1024,128]{1,0:T(8,128)(2,1)S(1)}, u32[]{:S(2)}, u32[]{:S(2)}) collective-permute-start(bf16[1024,128]{1,0:T(8,128)(2,1)} %rope_hbm.1), channel_id=1, source_target_pairs={{0,4},{4,0},{1,5},{5,1},{2,6},{6,2},{3,7},{7,3},{8,12},{12,8},{9,1... | collective-permute-start | bytes 786440 | tf_op jit(solution)/shard_map/ppermute | solution.py:327
  0.5 4.3 %collective-permute-start.2 = (bf16[128,128]{1,0:T(8,128)(2,1)}, bf16[128,128]{1,0:T(8,128)(2,1)S(1)}, u32[]{:S(2)}, u32[]{:S(2)}) collective-permute-start(bf16[128,128]{1,0:T(8,128)(2,1)} %bitcast.6), channel_id=1, source_target_pairs={{0,4},{4,0},{1,5},{5,1},{2,6},{6,2},{3,7},{7,3},{8,12},{12,8},{9,1... | collective-permute-start | bytes 98312 | tf_op jit(solution)/shard_map/ppermute | solution.py:327
  0.5 4.3 %copy-start.1 = (bf16[16,8,128]{2,1,0:T(8,128)(2,1)S(1)}, bf16[16,8,128]{2,1,0:T(8,128)(2,1)}, u32[]{:S(2)}) copy-start(bf16[16,8,128]{2,1,0:T(8,128)(2,1)} %param.14) | copy-start | bytes 98308
  7.4 50.0 %copy-start = (bf16[2048,112]{0,1:T(8,128)(2,1)S(1)}, bf16[2048,112]{0,1:T(8,128)(2,1)}, u32[]{:S(2)}) copy-start(bf16[2048,112]{0,1:T(8,128)(2,1)} %param.15) | copy-start | bytes 1376260
  7.4 7.5 %collective-permute-start.3 = (bf16[592,128]{1,0:T(8,128)(2,1)S(1)}, bf16[592,128]{1,0:T(8,128)(2,1)S(1)}, u32[]{:S(2)}, u32[]{:S(2)}) collective-permute-start(bf16[592,128]{1,0:T(8,128)(2,1)S(1)} %get-tuple-element.26), channel_id=1, source_target_pairs={{0,64},{64,128},{128,192},{192,0},{1,65},{65,129},{129,193},{193,1... | collective-permute-start | bytes 454664 | tf_op jit(solution)/shard_map/ppermute | solution.py:389
  9.1 10.4 %collective-permute-start.4 = (bf16[592,128]{1,0:T(8,128)(2,1)S(1)}, bf16[592,128]{1,0:T(8,128)(2,1)S(1)}, u32[]{:S(2)}, u32[]{:S(2)}) collective-permute-start(bf16[592,128]{1,0:T(8,128)(2,1)S(1)} %get-tuple-element.27), channel_id=1, source_target_pairs={{0,128},{64,192},{128,0},{192,64},{1,129},{65,193},{129,1},{193,65... | collective-permute-start | bytes 454664 | tf_op jit(solution)/shard_map/ppermute | solution.py:389
  12.0 7.5 %collective-permute-start.5 = (bf16[592,128]{1,0:T(8,128)(2,1)S(1)}, bf16[592,128]{1,0:T(8,128)(2,1)S(1)}, u32[]{:S(2)}, u32[]{:S(2)}) collective-permute-start(bf16[592,128]{1,0:T(8,128)(2,1)S(1)} %get-tuple-element.28), channel_id=1, source_target_pairs={{0,192},{64,0},{128,64},{192,128},{1,193},{65,1},{129,65},{193,129... | collective-permute-start | bytes 454664 | tf_op jit(solution)/shard_map/ppermute | solution.py:389
  56.1 1.3 %collective-permute-start.6 = (bf16[32,16,128]{2,1,0:T(8,128)(2,1)S(1)}, bf16[32,16,128]{2,1,0:T(8,128)(2,1)S(1)}, u32[]{:S(2)}, u32[]{:S(2)}) collective-permute-start(bf16[32,16,128]{2,1,0:T(8,128)(2,1)S(1)} %all_to_all.11.own), channel_id=1, source_target_pairs={{0,4},{4,0},{1,5},{5,1},{2,6},{6,2},{3,7},{7,3},{8,12},{12,8},{9,1... | collective-permute-start | bytes 393224 | tf_op jit(solution)/shard_map/ppermute | solution.py:409
  57.9 3.7 %collective-permute-start.7 = (f32[2,8,112]{2,1,0:T(8,128)S(1)}, f32[2,8,112]{2,1,0:T(8,128)S(1)}, u32[]{:S(2)}, u32[]{:S(2)}) collective-permute-start(f32[2,8,112]{2,1,0:T(8,128)S(1)} %get-tuple-element.30), channel_id=1, source_target_pairs={{0,1},{1,2},{2,3},{3,0},{4,5},{5,6},{6,7},{7,4},{8,9},{9,10},{10,1... | collective-permute-start | bytes 21512 | tf_op jit(solution)/shard_map/ppermute | solution.py:421
  58.4 5.2 %collective-permute-start.8 = (f32[2,8,112]{2,1,0:T(8,128)S(1)}, f32[2,8,112]{2,1,0:T(8,128)S(1)}, u32[]{:S(2)}, u32[]{:S(2)}) collective-permute-start(f32[2,8,112]{2,1,0:T(8,128)S(1)} %get-tuple-element.31), channel_id=1, source_target_pairs={{0,2},{1,3},{2,0},{3,1},{4,6},{5,7},{6,4},{7,5},{8,10},{9,11},{10,... | collective-permute-start | bytes 21512 | tf_op jit(solution)/shard_map/ppermute | solution.py:421
  60.8 4.9 %collective-permute-start.9 = (f32[2,8,112]{2,1,0:T(8,128)S(1)}, f32[2,8,112]{2,1,0:T(8,128)S(1)}, u32[]{:S(2)}, u32[]{:S(2)}) collective-permute-start(f32[2,8,112]{2,1,0:T(8,128)S(1)} %get-tuple-element.32), channel_id=1, source_target_pairs={{0,3},{1,0},{2,1},{3,2},{4,7},{5,4},{6,5},{7,6},{8,11},{9,8},{10,9... | collective-permute-start | bytes 21512 | tf_op jit(solution)/shard_map/ppermute | solution.py:421
